TPU v7x, 256 devices: a whole 4x4x8 slice. The times are simulated.
256 devices in a mesh: seq: 16 (over x, y), chan: 16 (over z, core).
Axes of the slice: x: 4, y: 4, z: 8, core: 2. Of those that a mesh axis runs over, the one named last changes fastest.
Arguments:
- tokens: bfloat16 [16384, 4096], P('seq', 'chan'), may hold values from -6 to 6
- w_in: bfloat16 [4096, 4096], P(None, 'chan'), may hold values from -0.09375 to 0.09375
- residues: float32 [4096, 16], P('chan'), may hold values from -2.25 to 2.25
- decays: float32 [4096, 16], P('chan'), may hold values from 1.8310547e-05 to 2
- skip_gain: float32 [4096], P('chan'), may hold values from -1.2 to 1.2
- w_out: bfloat16 [4096, 4096], P('chan'), may hold values from -0.125 to 0.125
Outputs:
- mixed: bfloat16 [16384, 4096], P('seq', 'chan')
All inputs are finite; a program needn't handle non-finite values.
Results may differ from a plain program's by a relative error of at most 0.03.
Values may be sent and summed in bfloat16 or wider, within the bound.
A program may use at most 128 MiB of HBM per device.

v0:
```python
import math

import jax
import jax.numpy as jnp
from jax import lax
from jax.sharding import PartitionSpec as P

PRECISE = lax.Precision.HIGHEST
transform_precision = lax.Precision.HIGH


def phases(numerator, period):
    angle = (numerator % period).astype(jnp.float32) * (2.0 * math.pi / period)
    return (jnp.cos(angle), jnp.sin(angle))


def complex_apply(form, mat_re, mat_im, vec_re, vec_im):
    real_part = jnp.einsum(form, mat_re, vec_re, precision=transform_precision) - jnp.einsum(
        form, mat_im, vec_im, precision=transform_precision
    )
    imag_part = jnp.einsum(form, mat_re, vec_im, precision=transform_precision) + jnp.einsum(
        form, mat_im, vec_re, precision=transform_precision
    )
    return (real_part, imag_part)


def split_length(length):
    first_len = math.isqrt(length)
    while length % first_len:
        first_len -= 1
    return first_len


def local_dft(vec_re, vec_im, sign):
    lead_dim, length, channels = vec_re.shape
    first_len = split_length(length)
    second_len = length // first_len
    index_one = jnp.arange(first_len, dtype=jnp.int32)
    index_two = jnp.arange(second_len, dtype=jnp.int32)
    cos_one, sin_one = phases(index_one[:, None] * index_one[None, :], first_len)
    part_re, part_im = complex_apply(
        "kj,ejbc->ekbc",
        cos_one,
        sign * sin_one,
        vec_re.reshape(lead_dim, first_len, second_len, channels),
        vec_im.reshape(lead_dim, first_len, second_len, channels),
    )
    cos_tw, sin_tw = phases(index_one[:, None] * index_two[None, :], length)
    sin_tw = sign * sin_tw
    turned_re = part_re * cos_tw[None, :, :, None] - part_im * sin_tw[None, :, :, None]
    turned_im = part_im * cos_tw[None, :, :, None] + part_re * sin_tw[None, :, :, None]
    cos_two, sin_two = phases(index_two[:, None] * index_two[None, :], second_len)
    out_re, out_im = complex_apply("mb,ekbc->emkc", cos_two, sign * sin_two, turned_re, turned_im)
    return (out_re.reshape(lead_dim, length, channels), out_im.reshape(lead_dim, length, channels))


def spectrum(freqs, period, filter_taps, residues, decays):
    _, sin_full = phases(freqs, period)
    _, sin_half = phases(freqs, 2 * period)
    sign_k = (1 - 2 * (freqs % 2)).astype(jnp.float32)

    def add_order(order_idx, totals):
        decay_rate = lax.dynamic_slice_in_dim(decays, order_idx, 1, 1)[:, 0]
        pole_gain = lax.dynamic_slice_in_dim(residues, order_idx, 1, 1)[:, 0] * jnp.sqrt(decay_rate)
        step_decay = jnp.exp(-decay_rate)
        numerator = 1.0 - sign_k[:, None] * jnp.exp(-decay_rate * filter_taps)[None, :]
        den_re = (
            -jnp.expm1(-decay_rate)[None, :]
            + 2.0 * step_decay[None, :] * (sin_half * sin_half)[:, None]
        )
        den_im = step_decay[None, :] * sin_full[:, None]
        weighting = pole_gain[None, :] * numerator / (den_re * den_re + den_im * den_im)
        return (totals[0] + weighting * den_re, totals[1] - weighting * den_im)

    zeros_acc = jnp.zeros((freqs.shape[0], residues.shape[0]), jnp.float32)
    return lax.fori_loop(0, residues.shape[1], add_order, (zeros_acc, zeros_acc))


def spectral_conv(stream, residues, decays):
    tok_rows, channels = stream.shape
    seq_parts = lax.axis_size("seq")
    group_rows = tok_rows // seq_parts
    period = 2 * seq_parts * tok_rows
    own_index = lax.axis_index("seq")
    blocks = lax.all_to_all(
        stream.reshape(seq_parts, group_rows, channels),
        "seq",
        split_axis=0,
        concat_axis=0,
        tiled=True,
    ).astype(jnp.float32)
    rows_a = jnp.arange(seq_parts, dtype=jnp.int32)
    rows_k = jnp.arange(2 * seq_parts, dtype=jnp.int32)
    cos_a, sin_a = phases(rows_k[:, None] * rows_a[None, :], 2 * seq_parts)
    freq_re = jnp.einsum("ka,agc->kgc", cos_a, blocks, precision=PRECISE)
    freq_im = -jnp.einsum("ka,agc->kgc", sin_a, blocks, precision=PRECISE)
    positions = own_index * group_rows + jnp.arange(group_rows, dtype=jnp.int32)
    cos_b, sin_b = phases(rows_k[:, None] * positions[None, :], period)
    turn_re = freq_re * cos_b[:, :, None] + freq_im * sin_b[:, :, None]
    turn_im = freq_im * cos_b[:, :, None] - freq_re * sin_b[:, :, None]
    turn_re, turn_im = (
        lax.all_to_all(
            turn_re.astype(jnp.bfloat16), "seq", split_axis=0, concat_axis=1, tiled=True
        ).astype(turn_re.dtype),
        lax.all_to_all(
            turn_im.astype(jnp.bfloat16), "seq", split_axis=0, concat_axis=1, tiled=True
        ).astype(turn_im.dtype),
    )
    spec_re, spec_im = local_dft(turn_re, turn_im, -1.0)
    pair_rows = own_index * 2 + jnp.arange(2, dtype=jnp.int32)
    freqs = (
        pair_rows[:, None] + 2 * seq_parts * jnp.arange(tok_rows, dtype=jnp.int32)[None, :]
    ).reshape(-1)
    filt_re, filt_im = spectrum(freqs, period, seq_parts * tok_rows, residues, decays)
    filt_re = filt_re.reshape(2, tok_rows, channels)
    filt_im = filt_im.reshape(2, tok_rows, channels)
    prod_re = spec_re * filt_re - spec_im * filt_im
    prod_im = spec_re * filt_im + spec_im * filt_re
    back_re, back_im = local_dft(prod_re, prod_im, 1.0)
    cos_c, sin_c = phases(
        pair_rows[:, None] * jnp.arange(tok_rows, dtype=jnp.int32)[None, :], period
    )
    turned_re = back_re * cos_c[:, :, None] - back_im * sin_c[:, :, None]
    turned_im = back_im * cos_c[:, :, None] + back_re * sin_c[:, :, None]
    turned_re, turned_im = (
        lax.all_to_all(
            turned_re.astype(jnp.bfloat16), "seq", split_axis=1, concat_axis=0, tiled=True
        ).astype(turned_re.dtype),
        lax.all_to_all(
            turned_im.astype(jnp.bfloat16), "seq", split_axis=1, concat_axis=0, tiled=True
        ).astype(turned_im.dtype),
    )
    cos_i, sin_i = phases(rows_a[:, None] * rows_k[None, :], 2 * seq_parts)
    values = jnp.einsum("ak,kgc->agc", cos_i, turned_re, precision=PRECISE) - jnp.einsum(
        "ak,kgc->agc", sin_i, turned_im, precision=PRECISE
    )
    values = values / period
    values = lax.all_to_all(
        values.astype(jnp.bfloat16), "seq", split_axis=0, concat_axis=0, tiled=True
    ).astype(values.dtype)
    return values.reshape(tok_rows, channels)


def per_device(tokens, w_in, residues, decays, skip_gain, w_out):
    stream = jnp.dot(
        lax.all_gather(tokens, "chan", axis=1, tiled=True), w_in, preferred_element_type=jnp.float32
    ).astype(jnp.bfloat16)
    long_part = spectral_conv(stream, residues, decays)
    conv = (long_part + skip_gain[None, :] * stream.astype(jnp.float32)).astype(jnp.bfloat16)
    mixed = (
        lax.psum_scatter(
            lax.dot_general(
                w_out, conv, (((0,), (1,)), ((), ())), preferred_element_type=jnp.float32
            ).astype(jnp.bfloat16),
            "chan",
            scatter_dimension=0,
            tiled=True,
        )
        .astype(jnp.float32)
        .T
    )
    return mixed.astype(jnp.bfloat16)


def solution(mesh):
    in_specs = (
        P("seq", "chan"),
        P(None, "chan"),
        P("chan", None),
        P("chan", None),
        P("chan"),
        P("chan", None),
    )
    out_specs = P("seq", "chan")
    return jax.shard_map(
        per_device, mesh=mesh, in_specs=in_specs, out_specs=out_specs, check_vma=False
    )
```

profile of v0, /device:TPU:6, one launch (start us, length us, event | category | flops | bytes accessed | tf_op | source)
XLA Modules:
  0.0 401.5 jit_solution(8994281132717817459)
XLA Ops:
  7.3 68.7 %all-gather.2.cloned.1.call-done = bf16[1024,4096]{1,0:T(8,128)(2,1)} async-done(((bf16[1024,256]{1,0:T(8,128)(2,1)}), bf16[1024,4096]{1,0:T(8,128)(2,1)}) %all-gather.2.cloned.1.call-update) | async-done | bytes 8388624 | tf_op jit(solution)/shard_map/all_gather | solution.py:146
  75.9 7.1 %convolution_convert_fusion = bf16[1024,256]{1,0:T(8,128)(2,1)} fusion(bf16[1024,4096]{1,0:T(8,128)(2,1)} %all-gather.2.cloned.1.call-done, bf16[4096,256]{1,0:T(8,128)(2,1)} %param.9), kind=kOutput, calls=%fused_computation.95 | convolution fusion | flops 2147745792 | bytes 11010048 | tf_op jit(solution)/shard_map/dot_general | solution.py:145
  83.0 7.3 %all-to-all-start = ((bf16[16,64,256]{2,1,0:T(8,128)(2,1)}), bf16[16,64,256]{2,1,0:T(8,128)(2,1)S(1)}, u32[]{:S(2)}, u32[]{:S(2)}) async-start(bf16[16,64,256]{2,1,0:T(8,128)(2,1)} %bitcast.2), calls=%async_computation | async-start | bytes 1048576 | tf_op jit(solution)/shard_map/all_to_all | solution.py:85
  90.5 9.7 %all-to-all-done = bf16[16,64,256]{2,1,0:T(8,128)(2,1)S(1)} async-done(((bf16[16,64,256]{2,1,0:T(8,128)(2,1)}), bf16[16,64,256]{2,1,0:T(8,128)(2,1)S(1)}, u32[]{:S(2)}, u32[]{:S(2)}) %all-to-all-start) | async-done | bytes 524320 | tf_op jit(solution)/shard_map/all_to_all | solution.py:85
  105.9 5.6 %all-to-all-start.1 = ((bf16[32,64,256]{2,1,0:T(8,128)(2,1)}), bf16[32,64,256]{2,1,0:T(8,128)(2,1)S(1)}, u32[]{:S(2)}, u32[]{:S(2)}) async-start(bf16[32,64,256]{2,1,0:T(8,128)(2,1)} %copy.81), calls=%async_computation.1 | async-start | bytes 2097152 | tf_op jit(solution)/shard_map/all_to_all | solution.py:102
  114.3 11.6 %all-to-all-done.1 = bf16[32,64,256]{2,1,0:T(8,128)(2,1)S(1)} async-done(((bf16[32,64,256]{2,1,0:T(8,128)(2,1)}), bf16[32,64,256]{2,1,0:T(8,128)(2,1)S(1)}, u32[]{:S(2)}, u32[]{:S(2)}) %all-to-all-start.1) | async-done | bytes 1048608 | tf_op jit(solution)/shard_map/all_to_all | solution.py:102
  125.9 6.2 %all-to-all-start.2 = ((bf16[32,64,256]{2,1,0:T(8,128)(2,1)}), bf16[32,64,256]{2,1,0:T(8,128)(2,1)}, u32[]{:S(2)}, u32[]{:S(2)}) async-start(bf16[32,64,256]{2,1,0:T(8,128)(2,1)} %copy.84), calls=%async_computation.2 | async-start | bytes 2097152 | tf_op jit(solution)/shard_map/all_to_all | solution.py:105
  132.1 85.7 %while.20 = (s32[]{:T(128)}, f32[2048,256]{1,0:T(8,128)}, f32[2048,256]{1,0:T(8,128)}, f32[256,16]{0,1:T(8,128)}, f32[256,16]{0,1:T(8,128)}, /*index=5*/s32[1024]{0:T(1024)S(1)}, s32[2]{0:T(128)S(1)}, s32[]{:T(128)}, s32[]{:T(128)}) while((s32[]{:T(128)}, f32[2048,256]{1,0:T(8,128)}, f32[2048,256]{1,0:T(8,128)}, ...), condition=%wide.region_1.2_spmd.clone.clone.clone, body=%wide.region_0.1_spmd.clone.clone.clone.sunk | while | flops 8475907 | bytes 8512627 | solution.py:76
  137.2 4.3 %fusion.268 = (f32[2048,256]{1,0:T(8,128)}, f32[2048,256]{1,0:T(8,128)}) fusion(f32[2048,256]{1,0:T(8,128)} %get-tuple-element.394, f32[2048]{0:T(1024)S(1)} %fusion.265, f32[256]{0:T(256)S(1)} %bitcast.214, f32[2048]{0:T(1024)S(1)} %bitcast.211, f32[256]{0:T(256)S(1)} %broadcast_multiply_fusion.3, f32[256]{0:T(256)S(1)} %bitcast.216, ...), kind=kLoop, calls=%fused_computation.7.clone.1 | loop fusion | flops 8388608 | bytes 8418305 | tf_op jit(solution)/shard_map/while/body/eval_jaxpr/sub | solution.py:73
  142.7 4.3 %fusion.268 = (f32[2048,256]{1,0:T(8,128)}, f32[2048,256]{1,0:T(8,128)}) fusion(f32[2048,256]{1,0:T(8,128)} %get-tuple-element.394, f32[2048]{0:T(1024)S(1)} %fusion.265, f32[256]{0:T(256)S(1)} %bitcast.214, f32[2048]{0:T(1024)S(1)} %bitcast.211, f32[256]{0:T(256)S(1)} %broadcast_multiply_fusion.3, f32[256]{0:T(256)S(1)} %bitcast.216, ...), kind=kLoop, calls=%fused_computation.7.clone.1 | loop fusion | flops 8388608 | bytes 8418305 | tf_op jit(solution)/shard_map/while/body/eval_jaxpr/sub | solution.py:73
  148.1 4.3 %fusion.268 = (f32[2048,256]{1,0:T(8,128)}, f32[2048,256]{1,0:T(8,128)}) fusion(f32[2048,256]{1,0:T(8,128)} %get-tuple-element.394, f32[2048]{0:T(1024)S(1)} %fusion.265, f32[256]{0:T(256)S(1)} %bitcast.214, f32[2048]{0:T(1024)S(1)} %bitcast.211, f32[256]{0:T(256)S(1)} %broadcast_multiply_fusion.3, f32[256]{0:T(256)S(1)} %bitcast.216, ...), kind=kLoop, calls=%fused_computation.7.clone.1 | loop fusion | flops 8388608 | bytes 8418305 | tf_op jit(solution)/shard_map/while/body/eval_jaxpr/sub | solution.py:73
  153.6 4.3 %fusion.268 = (f32[2048,256]{1,0:T(8,128)}, f32[2048,256]{1,0:T(8,128)}) fusion(f32[2048,256]{1,0:T(8,128)} %get-tuple-element.394, f32[2048]{0:T(1024)S(1)} %fusion.265, f32[256]{0:T(256)S(1)} %bitcast.214, f32[2048]{0:T(1024)S(1)} %bitcast.211, f32[256]{0:T(256)S(1)} %broadcast_multiply_fusion.3, f32[256]{0:T(256)S(1)} %bitcast.216, ...), kind=kLoop, calls=%fused_computation.7.clone.1 | loop fusion | flops 8388608 | bytes 8418305 | tf_op jit(solution)/shard_map/while/body/eval_jaxpr/sub | solution.py:73
  159.0 4.3 %fusion.268 = (f32[2048,256]{1,0:T(8,128)}, f32[2048,256]{1,0:T(8,128)}) fusion(f32[2048,256]{1,0:T(8,128)} %get-tuple-element.394, f32[2048]{0:T(1024)S(1)} %fusion.265, f32[256]{0:T(256)S(1)} %bitcast.214, f32[2048]{0:T(1024)S(1)} %bitcast.211, f32[256]{0:T(256)S(1)} %broadcast_multiply_fusion.3, f32[256]{0:T(256)S(1)} %bitcast.216, ...), kind=kLoop, calls=%fused_computation.7.clone.1 | loop fusion | flops 8388608 | bytes 8418305 | tf_op jit(solution)/shard_map/while/body/eval_jaxpr/sub | solution.py:73
  164.4 4.3 %fusion.268 = (f32[2048,256]{1,0:T(8,128)}, f32[2048,256]{1,0:T(8,128)}) fusion(f32[2048,256]{1,0:T(8,128)} %get-tuple-element.394, f32[2048]{0:T(1024)S(1)} %fusion.265, f32[256]{0:T(256)S(1)} %bitcast.214, f32[2048]{0:T(1024)S(1)} %bitcast.211, f32[256]{0:T(256)S(1)} %broadcast_multiply_fusion.3, f32[256]{0:T(256)S(1)} %bitcast.216, ...), kind=kLoop, calls=%fused_computation.7.clone.1 | loop fusion | flops 8388608 | bytes 8418305 | tf_op jit(solution)/shard_map/while/body/eval_jaxpr/sub | solution.py:73
  191.6 4.3 %fusion.268 = (f32[2048,256]{1,0:T(8,128)}, f32[2048,256]{1,0:T(8,128)}) fusion(f32[2048,256]{1,0:T(8,128)} %get-tuple-element.394, f32[2048]{0:T(1024)S(1)} %fusion.265, f32[256]{0:T(256)S(1)} %bitcast.214, f32[2048]{0:T(1024)S(1)} %bitcast.211, f32[256]{0:T(256)S(1)} %broadcast_multiply_fusion.3, f32[256]{0:T(256)S(1)} %bitcast.216, ...), kind=kLoop, calls=%fused_computation.7.clone.1 | loop fusion | flops 8388608 | bytes 8418305 | tf_op jit(solution)/shard_map/while/body/eval_jaxpr/sub | solution.py:73
  208.0 4.3 %fusion.268 = (f32[2048,256]{1,0:T(8,128)}, f32[2048,256]{1,0:T(8,128)}) fusion(f32[2048,256]{1,0:T(8,128)} %get-tuple-element.394, f32[2048]{0:T(1024)S(1)} %fusion.265, f32[256]{0:T(256)S(1)} %bitcast.214, f32[2048]{0:T(1024)S(1)} %bitcast.211, f32[256]{0:T(256)S(1)} %broadcast_multiply_fusion.3, f32[256]{0:T(256)S(1)} %bitcast.216, ...), kind=kLoop, calls=%fused_computation.7.clone.1 | loop fusion | flops 8388608 | bytes 8418305 | tf_op jit(solution)/shard_map/while/body/eval_jaxpr/sub | solution.py:73
  235.0 4.6 %fusion.28 = (f32[2,32,32,256]{3,1,2,0:T(8,128)S(1)}, f32[2,32,32,256]{3,1,2,0:T(8,128)S(1)}) fusion(f32[2,32,256,32]{2,3,1,0:T(8,128)S(1)} %fusion.48, f32[2,32,32,256]{3,2,1,0:T(8,128)S(1)} %bitcast.202, f32[2,32,32,256]{3,2,1,0:T(8,128)S(1)} %bitcast.201, f32[2,32,256,32]{2,3,1,0:T(8,128)S(1)} %fusion.40, f32[2,32,32,256]{3,1,2,0:T(8,128)S(1)} %get-tuple-element.316), kind=kOutput, calls=%fused_computation.56 | convolution fusion | flops 104348672 | bytes 14680064 | tf_op jit(solution)/shard_map/mb,ekbc->emkc/dot_general | solution.py:21
  260.4 7.2 %all-to-all-start.3 = ((bf16[2,1024,256]{2,0,1:T(2,128)(2,1)}), bf16[2,1024,256]{2,0,1:T(2,128)(2,1)S(1)}, u32[]{:S(2)}, u32[]{:S(2)}) async-start(bf16[2,1024,256]{2,0,1:T(2,128)(2,1)} %copy.106), calls=%async_computation.3 | async-start | bytes 2097152 | tf_op jit(solution)/shard_map/all_to_all | solution.py:126
  270.9 9.2 %all-to-all-done.3 = bf16[2,1024,256]{2,0,1:T(2,128)(2,1)S(1)} async-done(((bf16[2,1024,256]{2,0,1:T(2,128)(2,1)}), bf16[2,1024,256]{2,0,1:T(2,128)(2,1)S(1)}, u32[]{:S(2)}, u32[]{:S(2)}) %all-to-all-start.3) | async-done | bytes 1048608 | tf_op jit(solution)/shard_map/all_to_all | solution.py:126
  280.2 6.1 %all-to-all-start.4 = ((bf16[2,1024,256]{2,0,1:T(2,128)(2,1)}), bf16[2,1024,256]{2,0,1:T(2,128)(2,1)}, u32[]{:S(2)}, u32[]{:S(2)}) async-start(bf16[2,1024,256]{2,0,1:T(2,128)(2,1)} %copy.109), calls=%async_computation.4 | async-start | bytes 2097152 | tf_op jit(solution)/shard_map/all_to_all | solution.py:129
  290.8 8.3 %all-to-all-done.4 = bf16[2,1024,256]{2,0,1:T(2,128)(2,1)} async-done(((bf16[2,1024,256]{2,0,1:T(2,128)(2,1)}), bf16[2,1024,256]{2,0,1:T(2,128)(2,1)}, u32[]{:S(2)}, u32[]{:S(2)}) %all-to-all-start.4) | async-done | bytes 1048608 | tf_op jit(solution)/shard_map/all_to_all | solution.py:129
  306.8 13.3 %all_to_all.76 = bf16[16,64,256]{2,1,0:T(8,128)(2,1)S(1)} all-to-all(bf16[16,64,256]{2,1,0:T(8,128)(2,1)S(1)} %copy.112), channel_id=1, replica_groups=mesh['seq'=16,'chan'=16] {'seq'}, dimensions={0} | all-to-all | bytes 1048576 | tf_op jit(solution)/shard_map/all_to_all | solution.py:138
  320.1 6.7 %convert_bitcast_fusion = bf16[4096,1024]{0,1:T(8,128)(2,1)} fusion(bf16[256,4096]{1,0:T(8,128)(2,1)S(1)} %copy-done, bf16[1024,256]{1,0:T(8,128)(2,1)S(1)} %bitcast.210, bf16[1024,256]{1,0:T(8,128)(2,1)} %convolution_convert_fusion, f32[256]{0:T(256)S(1)} %copy-done.5), kind=kOutput, calls=%fused_computation.39 | convolution fusion | flops 2152988672 | bytes 11535360 | tf_op jit(solution)/shard_map/dot_general | solution.py:152
  326.8 67.6 %reduce-scatter.2.cloned.1.call-done = bf16[256,1024]{0,1:T(8,128)(2,1)} async-done(((bf16[4096,1024]{0,1:T(8,128)(2,1)}), bf16[256,1024]{0,1:T(8,128)(2,1)}) %reduce-scatter.2.cloned.1.call-update) | async-done | bytes 524304 | tf_op jit(solution)/shard_map/reduce_scatter | solution.py:151
  (185 shorter events, 113.7 us)
Async XLA Ops:
  6.5 313.6 %copy-start = (bf16[256,4096]{1,0:T(8,128)(2,1)S(1)}, bf16[256,4096]{1,0:T(8,128)(2,1)}, u32[]{:S(2)}) copy-start(bf16[256,4096]{1,0:T(8,128)(2,1)} %param.13) | copy-start | bytes 6291460
  6.5 69.4 %all-gather.2.cloned.1.call-start = ((), (), s32[]{:S(2)}) async-start(), calls=%async_computation.7 | async-start | bytes 8912896 | tf_op jit(solution)/shard_map/all_gather | solution.py:146
  83.0 17.2 %all-to-all-start = ((bf16[16,64,256]{2,1,0:T(8,128)(2,1)}), bf16[16,64,256]{2,1,0:T(8,128)(2,1)S(1)}, u32[]{:S(2)}, u32[]{:S(2)}) async-start(bf16[16,64,256]{2,1,0:T(8,128)(2,1)} %bitcast.2), calls=%async_computation | async-start | bytes 1048576 | tf_op jit(solution)/shard_map/all_to_all | solution.py:85
  105.9 20.0 %all-to-all-start.1 = ((bf16[32,64,256]{2,1,0:T(8,128)(2,1)}), bf16[32,64,256]{2,1,0:T(8,128)(2,1)S(1)}, u32[]{:S(2)}, u32[]{:S(2)}) async-start(bf16[32,64,256]{2,1,0:T(8,128)(2,1)} %copy.81), calls=%async_computation.1 | async-start | bytes 2097152 | tf_op jit(solution)/shard_map/all_to_all | solution.py:102
  125.9 6.2 %copy-start.4 = (bf16[32,64,256]{2,1,0:T(8,128)(2,1)}, bf16[32,64,256]{2,1,0:T(8,128)(2,1)S(1)}, u32[]{:S(2)}) copy-start(bf16[32,64,256]{2,1,0:T(8,128)(2,1)S(1)} %all-to-all-done.1) | copy-start | bytes 3145732
  125.9 96.4 %all-to-all-start.2 = ((bf16[32,64,256]{2,1,0:T(8,128)(2,1)}), bf16[32,64,256]{2,1,0:T(8,128)(2,1)}, u32[]{:S(2)}, u32[]{:S(2)}) async-start(bf16[32,64,256]{2,1,0:T(8,128)(2,1)} %copy.84), calls=%async_computation.2 | async-start | bytes 2097152 | tf_op jit(solution)/shard_map/all_to_all | solution.py:105
  223.6 1.6 copy-start.3
  232.5 2.5 copy-start.1
  232.5 2.5 copy-start.2
  260.4 19.7 %all-to-all-start.3 = ((bf16[2,1024,256]{2,0,1:T(2,128)(2,1)}), bf16[2,1024,256]{2,0,1:T(2,128)(2,1)S(1)}, u32[]{:S(2)}, u32[]{:S(2)}) async-start(bf16[2,1024,256]{2,0,1:T(2,128)(2,1)} %copy.106), calls=%async_computation.3 | async-start | bytes 2097152 | tf_op jit(solution)/shard_map/all_to_all | solution.py:126
  280.2 18.9 %all-to-all-start.4 = ((bf16[2,1024,256]{2,0,1:T(2,128)(2,1)}), bf16[2,1024,256]{2,0,1:T(2,128)(2,1)}, u32[]{:S(2)}, u32[]{:S(2)}) async-start(bf16[2,1024,256]{2,0,1:T(2,128)(2,1)} %copy.109), calls=%async_computation.4 | async-start | bytes 2097152 | tf_op jit(solution)/shard_map/all_to_all | solution.py:129
  286.3 108.2 %reduce-scatter.2.cloned.1.call-start = ((), (), s32[]{:S(2)}) async-start(), calls=%async_computation.8 | async-start | bytes 8912896 | tf_op jit(solution)/shard_map/reduce_scatter | solution.py:151
  304.7 15.4 %copy-start.5 = (f32[256]{0:T(256)S(1)}, f32[256]{0:T(256)}, u32[]{:S(2)}) copy-start(f32[256]{0:T(256)} %param.12) | copy-start | bytes 3076
Sparse Core Ops, SparseCore 0:
  9.1 66.7 all-gather.1
  326.9 67.4 reduce-scatter.1
where the time goes:
time: 409 us; the launch traced here: 401 us
  waiting for transfers between devices  176 us (43%)
  other arithmetic  87.3 us (21%)
  matrix products  54 us (13%)
  starting transfers between devices  32.7 us (8%)
  local copies, waits for them, and re-layouts  23.9 us (6%)
  between operations  13.9 us (3%)
  blocking collectives  13.3 us (3%)
    all_gather x1, waiting for transfers between devices, per_device(): lax.all_gather(tokens, 'chan', axis=1, tiled=True)  68.7 us
    reduce_scatter x1, waiting for transfers between devices, per_device(): lax.psum_scatter(lax.dot_general(w_out, conv, (((0,), (1,)), ((), ())), p...  67.6 us
    sub x16, other arithmetic, add_order(): return (totals[0] + weighting * den_re, totals[1] - weighting * den_im)  66.5 us
    all_to_all x1, blocking collectives, spectral_conv(): lax.all_to_all(values.astype(jnp.bfloat16), 'seq', split_axis=0, concat_a...  13.3 us
    mul x16, other arithmetic, add_order(): lax.dynamic_slice_in_dim(residues, order_idx, 1, 1)[:, 0]  11.7 us
    all_to_all x1, waiting for transfers between devices, spectral_conv(): lax.all_to_all(turn_re.astype(jnp.bfloat16), 'seq', split_axis=0, concat_...  11.6 us
    dot_general x4, matrix products, complex_apply(): jnp.einsum(form, mat_im, vec_re, precision=transform_precision)  10.5 us
    all_to_all x1, waiting for transfers between devices, spectral_conv(): lax.all_to_all(stream.reshape(seq_parts, group_rows, channels), 'seq', sp...  9.66 us
  transfers between devices with their start and end apart: 7, of which 6 were waited for; matrix products, arithmetic and copies ran while one was open for 25% of the time, Pallas kernels for 0%

commit v1 on v0

v1 whole, which is shorter than its diff:
```python
import functools

import jax
import jax.numpy as jnp
from jax import lax
from jax.experimental import pallas as pl
from jax.experimental.pallas import tpu as pltpu
from jax.sharding import PartitionSpec as P

MESH = pl.DeviceIdType.MESH
F32 = jnp.float32
BF16 = jnp.bfloat16
SUB = 8
LANES = 128
PIECES = 8


def kernel(
    nseq, nz, rows, width, order,
    tokens, w_in, residues, decays, skip, w_out, out,
    x_buf, wi_buf, wo_buf, acc, u_buf, conv, part, arrived, leaving,
    g_buf, d_buf, power, before, total, states, carry_in,
    ring_in, ring_out, pair_in, pair_out, sum_in, sum_out, state_in, state_out, conv_in, conv_out,
    wo_in, wo_sent, local,
):
    row = lax.axis_index("seq")
    chan = lax.axis_index("chan")
    z, core = chan // 2, chan % 2
    step_dir = 1 - 2 * core
    up = lax.rem(z + step_dir + nz, nz)
    down = lax.rem(z - step_dir + nz, nz)
    next_dev = {"chan": 2 * up + core}
    prev_dev = {"chan": 2 * down + core}
    twin = {"chan": 2 * z + 1 - core}
    half = rows // 2
    piece = rows // PIECES
    per_half = PIECES // 2
    span = half // SUB
    tiles = width // LANES

    barrier = pltpu.get_barrier_semaphore()
    for other in (next_dev, prev_dev, twin):
        pl.semaphore_signal(barrier, inc=1, device_id=other, device_id_type=MESH)

    def greet(step, _):
        other = lax.rem(row + step, nseq)
        pl.semaphore_signal(barrier, inc=1, device_id={"seq": other}, device_id_type=MESH)
        return 0

    lax.fori_loop(1, nseq, greet, 0)
    own_tokens = pltpu.make_async_copy(tokens, x_buf.at[chan], local.at[0])
    own_tokens.start()
    load_wi = pltpu.make_async_copy(w_in, wi_buf, local.at[1])
    load_wi.start()
    pl.semaphore_wait(barrier, nseq + 2)

    def block_of(step):
        mine = lax.rem(z - step_dir * step + 2 * nz, nz)
        theirs = lax.rem(z + step_dir * step + 2 * nz, nz)
        return 2 * mine + core, 2 * theirs + 1 - core

    def ring_copy(step, p, src_block, src=None):
        rows_p = pl.ds(p * piece, piece)
        src = x_buf.at[src_block, rows_p] if src is None else src.at[rows_p]
        return pltpu.make_async_remote_copy(
            src_ref=src, dst_ref=x_buf.at[src_block, rows_p],
            send_sem=ring_out.at[step, p], recv_sem=ring_in.at[step, p],
            device_id=next_dev, device_id_type=MESH)

    def pair_copy(step, p, src_block, src=None):
        rows_p = pl.ds(p * piece, piece)
        src = x_buf.at[src_block, rows_p] if src is None else src.at[rows_p]
        return pltpu.make_async_remote_copy(
            src_ref=src, dst_ref=x_buf.at[src_block, rows_p],
            send_sem=pair_out.at[step, p], recv_sem=pair_in.at[step, p],
            device_id=twin, device_id_type=MESH)

    def wo_copy(block):
        cols = pl.ds(pl.multiple_of((2 * block + 1 - core) * width, LANES), width)
        return pltpu.make_async_remote_copy(
            src_ref=w_out.at[:, cols], dst_ref=wo_buf.at[block, pl.ds(core * width, width)],
            send_sem=wo_sent.at[block], recv_sem=wo_in.at[block],
            device_id=twin, device_id_type=MESH)

    def wo_load(block):
        cols = pl.ds(pl.multiple_of((2 * block + core) * width, LANES), width)
        return pltpu.make_async_copy(
            w_out.at[:, cols], wo_buf.at[block, pl.ds(core * width, width)], local.at[2 + block])

    for p in range(per_half):
        ring_copy(0, p, chan, tokens).start()
    for p in range(per_half):
        pair_copy(0, p, chan, tokens).start()

    gain = residues[...] * jnp.sqrt(decays[...])
    g_buf[...] = gain.T
    d_buf[...] = decays[...].T
    place = lax.broadcasted_iota(jnp.int32, (SUB, width), 0).astype(F32)
    for r in range(order):
        power[r] = jnp.exp(-d_buf[r:r + 1] * (place * span))

    own_tokens.wait()
    load_wi.wait()

    def project(h, step, first):
        mine, theirs = block_of(step)
        rows_h = pl.ds(h * half, half)
        term = jnp.dot(x_buf[mine, rows_h], wi_buf[mine], preferred_element_type=F32)
        term += jnp.dot(x_buf[theirs, rows_h], wi_buf[theirs], preferred_element_type=F32)
        if first:
            acc[rows_h] = term
        else:
            acc[rows_h] += term

    def pair_wait(h, step):
        _, theirs = block_of(step)
        for p in range(h * per_half, (h + 1) * per_half):
            pair_copy(step, p, theirs).wait_recv()

    def ring_step(h, step):
        mine, _ = block_of(step)
        for p in range(h * per_half, (h + 1) * per_half):
            ring_copy(step - 1, p, mine).wait_recv()
            ring_copy(step, p, mine).start()
            pair_copy(step, p, mine).start()
        pair_wait(h, step)
        project(h, step, False)

    def last_step(h):
        mine, _ = block_of(nz - 1)
        for p in range(h * per_half, (h + 1) * per_half):
            ring_copy(nz - 2, p, mine).wait_recv()
            pair_copy(nz - 1, p, mine).start()
        pair_wait(h, nz - 1)
        project(h, nz - 1, False)
        rows_h = pl.ds(h * half, half)
        for tile in range(tiles):
            u_buf[tile, rows_h] = acc[rows_h, tile * LANES:(tile + 1) * LANES].astype(BF16).astype(F32)

    def steps(h, first, last):
        def body(step, _):
            ring_step(h, step)
            return 0
        lax.fori_loop(first, last, body, 0)

    def scan(h, tile):
        lanes = pl.ds(tile * LANES, LANES)
        a = [jnp.broadcast_to(jnp.exp(-d_buf[r:r + 1, lanes]), (SUB, LANES)) for r in range(order)]
        g = [jnp.broadcast_to(g_buf[r:r + 1, lanes], (SUB, LANES)) for r in range(order)]
        direct = jnp.broadcast_to(skip[:, lanes], (SUB, LANES))

        def body(i, hs):
            where = pl.ds(h * half + i, SUB, stride=span)
            u = u_buf[tile, where]
            hs = tuple(a[r] * hs[r] + g[r] * u for r in range(order))
            terms = [direct * u] + list(hs)
            while len(terms) > 1:
                terms = [terms[k] + terms[k + 1] if k + 1 < len(terms) else terms[k] for k in range(0, len(terms), 2)]
            u_buf[tile, where] = terms[0]
            return hs

        hs = lax.fori_loop(0, span, body, tuple(jnp.zeros((SUB, LANES), F32) for _ in range(order)))
        sub = lax.broadcasted_iota(jnp.int32, (SUB, LANES), 0)
        for r in range(order):
            run = hs[r]
            for shift in (1, 2, 4):
                factor = jnp.exp(-d_buf[r:r + 1, lanes] * float(span * shift))
                run = run + jnp.where(sub >= shift, factor * pltpu.roll(run, shift, 0), 0.0)
            before[h, r, :, lanes] = jnp.where(sub >= 1, pltpu.roll(run, 1, 0), 0.0)
            total[h, r:r + 1, lanes] = run[SUB - 1:SUB]

    def finish(h, tile):
        lanes = pl.ds(tile * LANES, LANES)
        a = [jnp.broadcast_to(jnp.exp(-d_buf[r:r + 1, lanes]), (SUB, LANES)) for r in range(order)]
        hs = tuple(
            before[h, r, :, lanes] + power[r, :, lanes] * carry_in[h, r:r + 1, lanes] for r in range(order))

        def body(i, hs):
            where = pl.ds(h * half + i, SUB, stride=span)
            hs = tuple(a[r] * hs[r] for r in range(order))
            terms = [u_buf[tile, where]] + list(hs)
            while len(terms) > 1:
                terms = [terms[k] + terms[k + 1] if k + 1 < len(terms) else terms[k] for k in range(0, len(terms), 2)]
            u_buf[tile, where] = terms[0]
            return hs

        lax.fori_loop(0, span, body, hs)

    pair_wait(0, 0)
    project(0, 0, True)
    steps(0, 1, nz - 1)
    for p in range(per_half, PIECES):
        ring_copy(0, p, chan, tokens).start()
    for p in range(per_half, PIECES):
        pair_copy(0, p, chan, tokens).start()
    last_step(0)
    pair_wait(1, 0)
    project(1, 0, True)
    for block in range(nz):
        wo_load(block).start()
        wo_copy(block).start()
    bounds = [1 + (k * (nz - 2)) // (tiles + 1) for k in range(tiles + 2)]
    for tile in range(tiles):
        steps(1, bounds[tile], bounds[tile + 1])
        scan(0, tile)
    steps(1, bounds[tiles], nz - 1)
    last_step(1)

    for tile in range(tiles):
        scan(1, tile)
    half_decay = jnp.exp(-d_buf[...] * float(half))
    states[row] = half_decay * total[0] + total[1]

    def state_copy(src, target):
        return pltpu.make_async_remote_copy(
            src_ref=states.at[src], dst_ref=states.at[src],
            send_sem=state_out.at[target], recv_sem=state_in.at[src],
            device_id={"seq": target}, device_id_type=MESH)

    def send_state(target, _):
        state_copy(row, target).start()
        return 0

    lax.fori_loop(row + 1, nseq, send_state, 0)
    block_decay = jnp.exp(-d_buf[...] * float(rows))

    def add_state(src, carry):
        state_copy(src, row).wait_recv()
        return block_decay * carry + states[src]

    carry = lax.fori_loop(0, row, add_state, jnp.zeros((order, width), F32))
    carry_in[0] = carry
    carry_in[1] = half_decay * carry + total[0]

    def conv_copy(h):
        rows_h = pl.ds(h * half, half)
        return pltpu.make_async_remote_copy(
            src_ref=conv.at[core, rows_h], dst_ref=conv.at[core, rows_h],
            send_sem=conv_out.at[h], recv_sem=conv_in.at[h], device_id=twin, device_id_type=MESH)

    def conv_from_twin(h):
        rows_h = pl.ds(h * half, half)
        return pltpu.make_async_remote_copy(
            src_ref=conv.at[1 - core, rows_h], dst_ref=conv.at[1 - core, rows_h],
            send_sem=conv_out.at[h], recv_sem=conv_in.at[h], device_id=twin, device_id_type=MESH)

    for h in range(2):
        for tile in range(tiles):
            finish(h, tile)
        rows_h = pl.ds(h * half, half)
        for tile in range(tiles):
            conv[core, rows_h, pl.ds(tile * LANES, LANES)] = u_buf[tile, rows_h].astype(BF16)
        conv_copy(h).start()

    for block in range(nz):
        wo_load(block).wait()
        wo_copy(block).wait_recv()

    def own_part(step, h):
        block = lax.rem(z - step_dir * (step + 1) + 2 * nz, nz)
        rows_h = pl.ds(h * half, half)
        part[rows_h] = jnp.dot(
            conv[0, rows_h], wo_buf[block, :width], preferred_element_type=F32) + jnp.dot(
            conv[1, rows_h], wo_buf[block, width:], preferred_element_type=F32)

    def sum_copy(step, p):
        rows_p = pl.ds(p * piece, piece)
        return pltpu.make_async_remote_copy(
            src_ref=leaving.at[step, rows_p], dst_ref=arrived.at[step, rows_p],
            send_sem=sum_out.at[step, p], recv_sem=sum_in.at[step, p],
            device_id=next_dev, device_id_type=MESH)

    for h in range(2):
        conv_from_twin(h).wait_recv()
        own_part(0, h)
        for p in range(h * per_half, (h + 1) * per_half):
            rows_p = pl.ds(p * piece, piece)
            leaving[0, rows_p] = part[rows_p].astype(BF16)
            sum_copy(0, p).start()

    def sum_step(step, _):
        for h in range(2):
            own_part(step, h)
        for p in range(PIECES):
            rows_p = pl.ds(p * piece, piece)
            sum_copy(step - 1, p).wait_recv()
            leaving[step, rows_p] = (arrived[step - 1, rows_p].astype(F32) + part[rows_p]).astype(BF16)
            sum_copy(step, p).start()
        return 0

    lax.fori_loop(1, nz - 1, sum_step, 0)
    for h in range(2):
        own_part(nz - 1, h)
    for p in range(PIECES):
        rows_p = pl.ds(p * piece, piece)
        sum_copy(nz - 2, p).wait_recv()
        out[rows_p] = (arrived[nz - 2, rows_p].astype(F32) + part[rows_p]).astype(BF16)

    def drain(step, _):
        for p in range(PIECES):
            ring_copy(step, p, chan).wait_send()
            pair_copy(step, p, chan).wait_send()
            sum_copy(step, p).wait_send()
        return 0

    lax.fori_loop(0, nz - 1, drain, 0)
    for p in range(PIECES):
        pair_copy(nz - 1, p, chan).wait_send()
    for block in range(nz):
        wo_copy(block).wait_send()
    for h in range(2):
        conv_copy(h).wait_send()

    def drain_state(target, _):
        state_copy(row, target).wait_send()
        return 0

    lax.fori_loop(row + 1, nseq, drain_state, 0)


def per_device(nseq, nchan, tokens, w_in, residues, decays, skip_gain, w_out):
    rows, width = tokens.shape
    order = residues.shape[1]
    nz = nchan // 2
    dma = pltpu.SemaphoreType.DMA
    vmem = pl.BlockSpec(memory_space=pltpu.VMEM)
    hbm = pl.BlockSpec(memory_space=pl.ANY)
    flops = 4 * rows * width * nchan * width
    return pl.pallas_call(
        functools.partial(kernel, nseq, nz, rows, width, order),
        out_shape=jax.ShapeDtypeStruct((rows, width), BF16),
        in_specs=[hbm, hbm, vmem, vmem, vmem, hbm],
        out_specs=vmem,
        scratch_shapes=[
            pltpu.VMEM((nchan, rows, width), BF16),
            pltpu.VMEM((nchan, width, width), BF16),
            pltpu.VMEM((nz, 2 * width, width), BF16),
            pltpu.VMEM((rows, width), F32),
            pltpu.VMEM((width // LANES, rows, LANES), F32),
            pltpu.VMEM((2, rows, width), BF16),
            pltpu.VMEM((rows, width), F32),
            pltpu.VMEM((nz - 1, rows, width), BF16),
            pltpu.VMEM((nz - 1, rows, width), BF16),
            pltpu.VMEM((order, width), F32),
            pltpu.VMEM((order, width), F32),
            pltpu.VMEM((order, SUB, width), F32),
            pltpu.VMEM((2, order, SUB, width), F32),
            pltpu.VMEM((2, order, width), F32),
            pltpu.VMEM((nseq, order, width), F32),
            pltpu.VMEM((2, order, width), F32),
            dma((nz - 1, PIECES)), dma((nz - 1, PIECES)),
            dma((nz, PIECES)), dma((nz, PIECES)),
            dma((nz - 1, PIECES)), dma((nz - 1, PIECES)),
            dma((nseq,)), dma((nseq,)),
            dma((2,)), dma((2,)),
            dma((nz,)), dma((nz,)),
            dma((2 + nz,)),
        ],
        compiler_params=pltpu.CompilerParams(
            collective_id=0, has_side_effects=True, vmem_limit_bytes=48 * 1024 * 1024),
        cost_estimate=pl.CostEstimate(flops=flops, bytes_accessed=6 * 1024 * 1024, transcendentals=0),
    )(tokens, w_in.reshape(nchan, width, width), residues, decays, skip_gain.reshape(1, width), w_out)


def solution(mesh):
    in_specs = (
        P("seq", "chan"),
        P(None, "chan"),
        P("chan", None),
        P("chan", None),
        P("chan"),
        P("chan", None),
    )
    return jax.shard_map(
        functools.partial(per_device, mesh.shape["seq"], mesh.shape["chan"]),
        mesh=mesh, in_specs=in_specs, out_specs=P("seq", "chan"), check_vma=False)
```

time: 409 us -> 130 us (0.32); the launches traced: 401 us -> 130 us
  waiting for transfers between devices: 176 us -> 0 us
  Pallas kernels: 0 us -> 122 us
  other arithmetic: 87.3 us -> 0 us
  matrix products: 54 us -> 0 us
  starting transfers between devices: 32.7 us -> 0 us
  local copies, waits for them, and re-layouts: 23.9 us -> 7.32 us
  between operations: 13.9 us -> 0.02 us
  blocking collectives: 13.3 us -> 0 us
    pallas_call x0 -> x1, Pallas kernels: none -> 122 us  [per_device(): pl.pallas_call(functools.partial(kernel, nseq, nz, rows, width, order), o...]
    all_gather x1 -> x0, waiting for transfers between devices: 68.7 us -> none  [per_device(): lax.all_gather(tokens, 'chan', axis=1, tiled=True)]
    reduce_scatter x1 -> x0, waiting for transfers between devices: 67.6 us -> none  [per_device(): lax.psum_scatter(lax.dot_general(w_out, conv, (((0,), (1,)), ((), ())), p...]
    sub x16 -> x0, other arithmetic: 66.5 us -> none  [add_order(): return (totals[0] + weighting * den_re, totals[1] - weighting * den_im)]
    dot_general x22 -> x0, matrix products: 54 us -> none  [the longest x4 10.5 us: complex_apply(): jnp.einsum(form, mat_im, vec_re, precision=transform_precision)]
    all_to_all x5 -> x0, waiting for transfers between devices: 38.7 us -> none  [the longest x1 11.6 us: spectral_conv(): lax.all_to_all(turn_re.astype(jnp.bfloat16), 'seq', split_axis=0, concat_...]
    all_to_all x5 -> x0, starting transfers between devices: 32.4 us -> none  [the longest x1 7.27 us: spectral_conv(): lax.all_to_all(stream.reshape(seq_parts, group_rows, channels), 'seq', sp...]
    mul x50 -> x0, other arithmetic: 16 us -> none  [the longest x16 11.7 us: add_order(): lax.dynamic_slice_in_dim(residues, order_idx, 1, 1)[:, 0]]
  transfers between devices with their start and end apart: 7 -> 0, of which waited for: 6 -> 0; matrix products, arithmetic and copies ran while one was open for 25% -> 0% of each run, Pallas kernels for 0% -> 0%
where the time goes in v1:
time: 130 us
  Pallas kernels  122 us (94%)
  local copies, waits for them, and re-layouts  7.32 us (6%)
    pallas_call x1, Pallas kernels, per_device(): pl.pallas_call(functools.partial(kernel, nseq, nz, rows, width, order), o...  122 us
    unnamed x11, local copies, waits for them, and re-layouts  7.32 us

profile of v1, /device:TPU:6, one launch (start us, length us, event | category | flops | bytes accessed | tf_op | source)
XLA Modules:
  0.0 129.7 jit_solution(18228717995891484060)
XLA Ops:
  0.0 0.8 copy.7.residues
  0.8 0.8 copy.8.decays
  1.6 0.0 copy-start
  1.6 1.6 %copy-done = bf16[4096,256]{1,0:T(8,128)(2,1)S(1)} copy-done((bf16[4096,256]{1,0:T(8,128)(2,1)S(1)}, bf16[4096,256]{1,0:T(8,128)(2,1)}, u32[]{:S(2)}) %copy-start) | copy-done | bytes 2097176
  3.2 0.0 copy-start.1
  3.2 1.6 %copy-done.1 = bf16[256,4096]{1,0:T(8,128)(2,1)S(1)} copy-done((bf16[256,4096]{1,0:T(8,128)(2,1)S(1)}, bf16[256,4096]{1,0:T(8,128)(2,1)}, u32[]{:S(2)}) %copy-start.1) | copy-done | bytes 2097176
  4.8 0.0 copy-start.2
  4.8 1.0 copy-done.2
  5.9 0.0 copy-start.3
  5.9 0.7 copy-done.3
  6.5 122.4 %shard_map.64 = bf16[1024,256]{1,0:T(8,128)(2,1)S(1)} custom-call(bf16[1024,256]{1,0:T(8,128)(2,1)S(1)} %copy-done.2, bf16[16,256,256]{2,1,0:T(8,128)(2,1)S(1)} %bitcast.2, f32[256,16]{1,0:T(8,128)S(1)} %copy.7.residues, f32[256,16]{1,0:T(8,128)S(1)} %copy.8.decays, f32[1,256]{1,0:T(1,128)S(1)} %bitcast.3, bf16[256,4096]{1,0:T(8,128)(2,1)S(1)} %copy-done.1), custom_call_target="tpu_custom_call" | custom-call | flops 4294967296 | bytes 6291456 | tf_op jit(solution)/shard_map/pallas_call | solution.py:329
  128.9 0.8 copy.10
Async XLA Ops:
  1.6 1.6 %copy-start = (bf16[4096,256]{1,0:T(8,128)(2,1)S(1)}, bf16[4096,256]{1,0:T(8,128)(2,1)}, u32[]{:S(2)}) copy-start(bf16[4096,256]{1,0:T(8,128)(2,1)} %param.7) | copy-start | bytes 6291460
  3.2 1.6 %copy-start.1 = (bf16[256,4096]{1,0:T(8,128)(2,1)S(1)}, bf16[256,4096]{1,0:T(8,128)(2,1)}, u32[]{:S(2)}) copy-start(bf16[256,4096]{1,0:T(8,128)(2,1)} %w_out.1) | copy-start | bytes 6291460
  4.8 1.0 copy-start.2
  5.9 0.7 copy-start.3

commit v2 on v0

v2 whole, which is shorter than its diff:
```python
import functools

import jax
import jax.numpy as jnp
from jax import lax
from jax.experimental import pallas as pl
from jax.experimental.pallas import tpu as pltpu
from jax.sharding import PartitionSpec as P

MESH = pl.DeviceIdType.MESH
F32 = jnp.float32
BF16 = jnp.bfloat16
SUB = 8
LANES = 128
UNROLL = 8
LAG = 4
NX = 4
WI_FIRST, WI_SECOND, WO_START, WO_FIRST, WO_SECOND, WI_DONE = 3, 6, 6, 10, 13, 13


def hop_counts(nz):
    group = nz // 2
    up, down = {}, {}
    for r in range(nz):
        last = r + group - 1
        if r == 0:
            up[r], down[r] = last, 0
        elif last >= nz:
            up[r], down[r] = last - nz, nz - r
        elif last < nz - r:
            up[r], down[r] = last, 0
        else:
            up[r], down[r] = 0, nz - r
    return up, down


def schedule(lengths):
    left = {r: n for r, n in lengths.items() if n > 0}
    ready = {r: 0 for r in left}
    items, place = [], 0
    while left:
        able = [r for r in left if ready[r] <= place]
        if able:
            r = max(able, key=lambda r: (left[r], -r))
            items.append((r, lengths[r] - left[r] + 1))
            left[r] -= 1
            ready[r] = place + LAG
            if left[r] == 0:
                del left[r]
        place += 1
    return items


def paths(nz):
    up, down = hop_counts(nz)
    first = schedule(up)
    mirror = {r: (nz // 2 + 1 - r) % nz for r in range(nz)}
    second = [(mirror[r], h) for r, h in first]
    assert sorted(second) == sorted((r, h) for r in down for h in range(1, down[r] + 1))
    return up, down, (first, second)


def kernel(
    nseq, nz, rows, width, order,
    tokens, w_in, residues, decays, skip, w_out, out,
    x_buf, relay, wi_a, wi_b, wo_a, wo_b, acc, u_buf, conv, part, arrived, leaving,
    far_res, far_dec, far_skip, g_buf, d_buf, k_buf, power, before, last, tail, states, carries, pair_last,
    ring_in, ring_out, pair_in, pair_out, own_in, own_out, sum_in, sum_out, state_in, state_out, conv_in, conv_out,
    wo_in, wo_sent, far_in, far_out, line_in, line_out, prm_in, prm_out, join_in, join_out, local,
):
    row = lax.axis_index("seq")
    chan = lax.axis_index("chan")
    z, core = chan // 2, chan % 2
    ny = nseq // NX
    x, y = row // ny, row % ny
    group = nz // 2
    sub = rows // nz
    mine = group * sub
    span = mine // SUB
    wide = 2 * width
    tiles = wide // LANES
    per_slot = SUB // group
    up, down, lists = paths(nz)
    count = len(lists[0])
    index = [{item: n for n, item in enumerate(items)} for items in lists]
    way = (1, -1)

    def at(dz, c):
        return {"chan": 2 * lax.rem(z + dz + nz, nz) + c}

    ring_dev = [at(1, core), at(nz - 1, core)]
    twin = at(0, 1 - core)
    partner = at(group, core)
    across = at(group, 1 - core)

    barrier = pltpu.get_barrier_semaphore()
    for other in (ring_dev[0], ring_dev[1], twin, partner, across):
        pl.semaphore_signal(barrier, inc=1, device_id=other, device_id_type=MESH)

    def greet(step, _):
        pl.semaphore_signal(
            barrier, inc=1, device_id={"seq": lax.rem(row + step, nseq)}, device_id_type=MESH)
        return 0

    lax.fori_loop(1, nseq, greet, 0)

    def remote(src, dst, send, recv, device):
        return pltpu.make_async_remote_copy(
            src_ref=src, dst_ref=dst, send_sem=send, recv_sem=recv, device_id=device, device_id_type=MESH)

    def slot_of(side, r, h):
        j = (way[side] * h - r) % nz
        return group - 1 - j if j < group else None

    def source_block(side, h, c):
        return 2 * lax.rem(z - way[side] * h + 2 * nz, nz) + c

    def slot_rows(k):
        return pl.ds(k * sub, sub)

    relays = [[item for item in lists[side] if slot_of(side, *item) is None] for side in (0, 1)]

    def place_of(side, r, h, block):
        k = slot_of(side, r, h)
        if k is None:
            return relay.at[side, relays[side].index((r, h))]
        return x_buf.at[block, slot_rows(k)]

    def own_rows(r):
        q = lax.rem(z + r, nz)
        return pl.ds(pl.multiple_of(q * sub, sub), sub)

    def ring_copy(side, r, h):
        block = source_block(side, h - 1, core)
        src = tokens.at[own_rows(r)] if h == 1 else place_of(side, r, h - 1, block)
        n = index[side][(r, h)]
        return remote(src, place_of(side, r, h, block), ring_out.at[side, n], ring_in.at[side, n], ring_dev[side])

    def pair_copy(side, r, h, from_twin=False):
        block = source_block(side, h, 1 - core if from_twin else core)
        ref = place_of(side, r, h, block)
        n = index[side][(r, h)]
        return remote(ref, ref, pair_out.at[side, n], pair_in.at[side, n], twin)

    own_parts = [r for r in range(nz) if (-r) % nz < group]

    def own_slot(r):
        return group - 1 - (-r) % nz

    def own_load(n):
        r = own_parts[n]
        return pltpu.make_async_copy(
            tokens.at[own_rows(r)], x_buf.at[chan, slot_rows(own_slot(r))], local.at[n])

    def own_pair(n):
        r = own_parts[n]
        return remote(
            tokens.at[own_rows(r)], x_buf.at[chan, slot_rows(own_slot(r))], own_out.at[n], own_in.at[n], twin)

    wi_load = pltpu.make_async_copy(w_in, wi_a, local.at[group])

    far_wi = remote(w_in.at[row], wi_b.at[x, y], far_out.at[0], far_in.at[0], partner)

    def far_wo(c):
        cols = pl.ds(pl.multiple_of((2 * (row // 2) + c) * width, LANES), width)
        device = {"chan": 2 * lax.rem(z + group, nz) + c}
        return remote(w_out.at[:, cols], wo_b.at[x, y], far_out.at[1 + c], far_in.at[1], device)

    def lines(which, stage):
        buf = (wi_b, wo_b)[which]
        low, high = pl.ds(0, width // 2), pl.ds(width // 2, width // 2)
        copies = []
        for step in range(1, NX):
            n = (step - 1, which, stage)
            device = {"seq": lax.rem(x + step, NX) * ny + y}
            ref = buf.at[x, y, low] if stage == 0 else buf.at[x, :, high]
            copies.append(remote(ref, ref, line_out.at[n], line_in.at[n], device))
        for step in range(1, ny):
            n = (NX - 1 + step - 1, which, stage)
            device = {"seq": x * ny + lax.rem(y + step, ny)}
            ref = buf.at[x, y, high] if stage == 0 else buf.at[:, y, low]
            copies.append(remote(ref, ref, line_out.at[n], line_in.at[n], device))
        return copies

    params = [
        remote(src, dst, prm_out.at[n], prm_in.at[n], partner)
        for n, (src, dst) in enumerate(((residues, far_res), (decays, far_dec), (skip, far_skip)))]

    def wo_cols(block, c):
        return pl.ds(pl.multiple_of((2 * block + c) * width, LANES), width)

    def wo_copy(block):
        return remote(
            w_out.at[:, wo_cols(block, 1 - core)], wo_a.at[block, pl.ds(core * width, width)],
            wo_sent.at[block], wo_in.at[block], twin)

    def wo_load(block):
        return pltpu.make_async_copy(
            w_out.at[:, wo_cols(block, core)], wo_a.at[block, pl.ds(core * width, width)],
            local.at[group + 1 + block])

    def project(delta, ab, first):
        total = None
        source = lax.rem(z - delta + nz, nz)
        for c in range(2):
            block = 2 * source + c
            weights = wi_a[block] if ab == 0 else wi_b[block // ny, lax.rem(block, ny)]
            term = jnp.dot(x_buf[block], weights, preferred_element_type=F32)
            total = term if total is None else total + term
        cols = pl.ds(ab * width, width)
        if first:
            acc[:, cols] = total
        else:
            acc[:, cols] += total

    for n in range(group):
        own_load(n).start()
    wi_load.start()
    pl.semaphore_wait(barrier, nseq + 4)
    far_wi.start()
    for side in (0, 1):
        ring_copy(side, *lists[side][0]).start()
    for copy in params:
        copy.start()
    for n in range(group):
        own_pair(n).start()

    sources = {}
    for side in (0, 1):
        for n, (r, h) in enumerate(lists[side]):
            if slot_of(side, r, h) is not None:
                sources.setdefault((way[side] * h) % nz, []).append((side, r, h, n))
    whole = {delta: max(n for _, _, _, n in got) + LAG + 1 for delta, got in sources.items()}

    arrived_items, fresh = set(), []

    def arrive(side, r, h):
        if (side, r, h) not in arrived_items:
            arrived_items.add((side, r, h))
            fresh.append((side, r, h))
            ring_copy(side, r, h).wait_recv()

    far_ready = False
    projected = []
    for step in range(max(count + LAG + 2, WI_DONE + 1)):
        for side in (0, 1):
            if 0 < step < count:
                r, h = lists[side][step]
                if h > 1:
                    arrive(side, r, h - 1)
                ring_copy(side, r, h).start()
        for side in (0, 1):
            if LAG <= step < count + LAG:
                arrive(side, *lists[side][step - LAG])
            for item in list(fresh):
                fresh.remove(item)
                if slot_of(*item) is not None:
                    pair_copy(*item).start()
        if step == 1:
            for block in range(nz):
                wo_load(block).start()
                wo_copy(block).start()
        if step == 2:
            for n in range(group):
                own_load(n).wait()
                own_pair(n).wait_recv()
            wi_load.wait()
            project(0, 0, True)
            projected.append(0)
        if step == WO_START:
            @pl.when(core == lax.rem(row, 2))
            def _():
                for c in range(2):
                    far_wo(c).start()
        if step == WI_FIRST:
            far_wi.wait_recv()
            for copy in lines(0, 0):
                copy.start()
        if step == WI_SECOND:
            for copy in lines(0, 0):
                copy.wait_recv()
            for copy in lines(0, 1):
                copy.start()
        if step == WO_FIRST:
            far_wo(0).wait_recv()
            for copy in lines(1, 0):
                copy.start()
        if step == WO_SECOND:
            for copy in lines(1, 0):
                copy.wait_recv()
            for copy in lines(1, 1):
                copy.start()
        if step == WI_DONE:
            for copy in lines(0, 1):
                copy.wait_recv()
            far_ready = True
            for n, delta in enumerate(projected):
                project(delta, 1, n == 0)
            for copy in params:
                copy.wait_recv()
            near, far = pl.ds(0, width), pl.ds(width, width)
            g_buf[:, near] = residues[...] * jnp.sqrt(decays[...])
            g_buf[:, far] = far_res[...] * jnp.sqrt(far_dec[...])
            d_buf[:, near] = decays[...]
            d_buf[:, far] = far_dec[...]
            k_buf[:, near] = skip[...]
            k_buf[:, far] = far_skip[...]
        for delta, ready in whole.items():
            if ready == step:
                for side, r, h, _ in sources[delta]:
                    pair_copy(side, r, h, True).wait_recv()
                project(delta, 0, False)
                if far_ready:
                    project(delta, 1, False)
                projected.append(delta)
    assert far_ready and len(projected) == nz
    for tile in range(tiles):
        u_buf[tile] = acc[:, tile * LANES:(tile + 1) * LANES].astype(BF16).astype(F32)

    low_chip = z < group
    cut = jnp.where(low_chip, per_slot * (group - 1 - z), 0)
    sub_id = lax.broadcasted_iota(jnp.int32, (SUB, LANES), 0)
    away = (sub_id - jnp.where(sub_id >= cut, cut, 0)).astype(F32) * float(span)

    def combine(terms):
        while len(terms) > 1:
            terms = [terms[k] + terms[k + 1] if k + 1 < len(terms) else terms[k] for k in range(0, len(terms), 2)]
        return terms[0]

    def scan(tile):
        lanes = pl.ds(tile * LANES, LANES)
        a = [jnp.broadcast_to(jnp.exp(-d_buf[r:r + 1, lanes]), (SUB, LANES)) for r in range(order)]
        g = [jnp.broadcast_to(g_buf[r:r + 1, lanes], (SUB, LANES)) for r in range(order)]
        direct = jnp.broadcast_to(k_buf[:, lanes], (SUB, LANES))

        def body(i, hs):
            where = pl.ds(i, SUB, stride=span)
            u = u_buf[tile, where]
            hs = tuple(a[r] * hs[r] + g[r] * u for r in range(order))
            u_buf[tile, where] = combine([direct * u] + list(hs))
            return hs

        hs = lax.fori_loop(
            0, span, body, tuple(jnp.zeros((SUB, LANES), F32) for _ in range(order)), unroll=UNROLL)
        for r in range(order):
            run = hs[r]
            for shift in (1, 2, 4):
                factor = jnp.exp(-d_buf[r:r + 1, lanes] * float(span * shift))
                joined = (sub_id >= shift) & ((sub_id < cut) | (sub_id - shift >= cut))
                run = run + jnp.where(joined, factor * pltpu.roll(run, shift, 0), 0.0)
            joined = (sub_id >= 1) & (sub_id != cut)
            before[r, :, lanes] = jnp.where(joined, pltpu.roll(run, 1, 0), 0.0)
            last[r:r + 1, lanes] = run[SUB - 1:SUB]
            tail[r:r + 1, lanes] = jnp.sum(jnp.where(sub_id == cut - 1, run, 0.0), axis=0, keepdims=True)

    for tile in range(tiles):
        scan(tile)

    def decay_over(parts):
        return jnp.exp(-d_buf[...] * (parts * sub).astype(F32))

    states[row] = decay_over(nz - 1 - z) * last[...] + tail[...]

    def state_copy(src, target):
        return remote(
            states.at[src], states.at[src], state_out.at[target], state_in.at[src], {"seq": target})

    def send_state(target, _):
        state_copy(row, target).start()
        return 0

    lax.fori_loop(row + 1, nseq, send_state, 0)
    join_last = remote(last, pair_last, join_out.at[0], join_in.at[0], partner)
    join_carry = remote(carries.at[0], carries.at[1], join_out.at[1], join_in.at[1], partner)
    join_last.start()
    for tile in range(tiles):
        lanes = pl.ds(tile * LANES, LANES)
        for r in range(order):
            power[r, :, lanes] = jnp.exp(-d_buf[r:r + 1, lanes] * away)
    block_decay = jnp.exp(-d_buf[...] * float(rows))

    def add_state(src, carry):
        state_copy(src, row).wait_recv()
        return block_decay * carry + states[src]

    carries[0] = lax.fori_loop(0, row, add_state, jnp.zeros((order, wide), F32))
    join_carry.start()
    to_middle = decay_over(jnp.where(low_chip, z + 1, z - group + 1))
    to_end = jnp.exp(-d_buf[...] * float(group * sub))
    join_last.wait_recv()
    join_carry.wait_recv()

    def swapped(value):
        return jnp.concatenate([value[:, width:], value[:, :width]], axis=1)

    theirs = swapped(pair_last[...])
    carry = carries[0] + swapped(carries[1])
    middle = to_middle * carry + jnp.where(low_chip, last[...], theirs)
    carries[2] = jnp.where(low_chip, carry, middle)
    carries[3] = to_end * middle + theirs

    def finish(tile):
        lanes = pl.ds(tile * LANES, LANES)
        a = [jnp.broadcast_to(jnp.exp(-d_buf[r:r + 1, lanes]), (SUB, LANES)) for r in range(order)]
        hs = tuple(
            before[r, :, lanes] + power[r, :, lanes] * jnp.where(
                sub_id >= cut, carries[2, r:r + 1, lanes], carries[3, r:r + 1, lanes])
            for r in range(order))

        def body(i, hs):
            where = pl.ds(i, SUB, stride=span)
            hs = tuple(a[r] * hs[r] for r in range(order))
            u_buf[tile, where] = combine([u_buf[tile, where]] + list(hs))
            return hs

        lax.fori_loop(0, span, body, hs, unroll=UNROLL)

    def conv_copy(ab, c):
        return remote(conv.at[c, ab], conv.at[c, ab], conv_out.at[ab], conv_in.at[ab], twin)

    per_ab = width // LANES
    for ab in range(2):
        for tile in range(per_ab):
            finish(ab * per_ab + tile)
            conv[core, ab, :, pl.ds(tile * LANES, LANES)] = u_buf[ab * per_ab + tile].astype(BF16)
        conv_copy(ab, core).start()

    def part_terms(delta, c):
        block = lax.rem(z - delta + nz, nz)
        share = 2 * block + c
        return jnp.dot(
            conv[c, 0], wo_a[block, pl.ds(c * width, width)], preferred_element_type=F32) + jnp.dot(
            conv[c, 1], wo_b[share // ny, lax.rem(share, ny)], preferred_element_type=F32)

    for block in range(nz):
        wo_load(block).wait()
        wo_copy(block).wait_recv()
    for copy in lines(1, 1):
        copy.wait_recv()
    for ab in range(2):
        conv_copy(ab, 1 - core).wait_recv()

    def target_of(side, r, i):
        length = (up, down)[side][r]
        h = length - i + 1
        return (way[side] * h) % nz, slot_of(side, r, h)

    def sum_copy(side, r, i):
        n = index[side][(r, i)]
        delta, k = target_of(side, r, i)
        src = arrived.at[side, index[side][(r, i - 1)]] if k is None else leaving.at[side, n]
        return remote(src, arrived.at[side, n], sum_out.at[side, n], sum_in.at[side, n], ring_dev[1 - side])

    have = set()

    def need(delta):
        if delta not in have:
            have.add(delta)
            part[delta] = part_terms(delta, 0) + part_terms(delta, 1)

    def finish_sum(r):
        total = None
        if (-r) % nz < group:
            need(0)
            total = part[0, own_rows_of_slot(own_slot(r))]
        for side in (0, 1):
            length = (up, down)[side][r]
            if length > 0:
                sum_copy(side, r, length).wait_recv()
                got = arrived[side, index[side][(r, length)]].astype(F32)
                total = got if total is None else total + got
        out[own_rows(r)] = total.astype(BF16)

    def own_rows_of_slot(k):
        return slot_rows(k)

    ends = {r: max([index[s][(r, (up, down)[s][r])] for s in (0, 1) if (up, down)[s][r] > 0] + [0]) + LAG for r in range(nz)}
    for step in range(count + LAG + 1):
        for side in (0, 1):
            if step < count:
                r, i = lists[side][step]
                delta, k = target_of(side, r, i)
                if k is not None:
                    need(delta)
                if i > 1:
                    sum_copy(side, r, i - 1).wait_recv()
                if k is not None:
                    value = part[delta, slot_rows(k)]
                    if i > 1:
                        value = value + arrived[side, index[side][(r, i - 1)]].astype(F32)
                    leaving[side, index[side][(r, i)]] = value.astype(BF16)
                sum_copy(side, r, i).start()
        for r in range(nz):
            if ends[r] == step:
                finish_sum(r)

    for side in (0, 1):
        for item in lists[side]:
            ring_copy(side, *item).wait_send()
            sum_copy(side, *item).wait_send()
            if slot_of(side, *item) is not None:
                pair_copy(side, *item).wait_send()
    for n in range(group):
        own_pair(n).wait_send()
    far_wi.wait_send()

    @pl.when(core == lax.rem(row, 2))
    def _():
        for c in range(2):
            far_wo(c).wait_send()

    for which in range(2):
        for stage in range(2):
            for copy in lines(which, stage):
                copy.wait_send()
    for copy in params:
        copy.wait_send()
    for block in range(nz):
        wo_copy(block).wait_send()
    join_last.wait_send()
    join_carry.wait_send()
    for ab in range(2):
        conv_copy(ab, core).wait_send()

    def drain_state(target, _):
        state_copy(row, target).wait_send()
        return 0

    lax.fori_loop(row + 1, nseq, drain_state, 0)


def per_device(nseq, nchan, tokens, w_in, residues, decays, skip_gain, w_out):
    rows, width = tokens.shape
    order = residues.shape[1]
    nz = nchan // 2
    ny = nseq // NX
    group = nz // 2
    mine = rows // 2
    wide = 2 * width
    count = len(paths(nz)[2][0])
    dma = pltpu.SemaphoreType.DMA
    vmem = pl.BlockSpec(memory_space=pltpu.VMEM)
    hbm = pl.BlockSpec(memory_space=pl.ANY)
    flops = 4 * rows * width * nchan * width
    return pl.pallas_call(
        functools.partial(kernel, nseq, nz, rows, width, order),
        out_shape=jax.ShapeDtypeStruct((rows, width), BF16),
        in_specs=[hbm, hbm, vmem, vmem, vmem, hbm],
        out_specs=vmem,
        scratch_shapes=[
            pltpu.VMEM((nchan, mine, width), BF16),
            pltpu.VMEM((2, 1, rows // nz, width), BF16),
            pltpu.VMEM((nchan, width, width), BF16),
            pltpu.VMEM((NX, ny, width, width), BF16),
            pltpu.VMEM((nz, 2 * width, width), BF16),
            pltpu.VMEM((NX, ny, width, width), BF16),
            pltpu.VMEM((mine, wide), F32),
            pltpu.VMEM((wide // LANES, mine, LANES), F32),
            pltpu.VMEM((2, 2, mine, width), BF16),
            pltpu.VMEM((nz, mine, width), F32),
            pltpu.VMEM((2, count, rows // nz, width), BF16),
            pltpu.VMEM((2, count, rows // nz, width), BF16),
            pltpu.VMEM((order, width), F32),
            pltpu.VMEM((order, width), F32),
            pltpu.VMEM((1, width), F32),
            pltpu.VMEM((order, wide), F32),
            pltpu.VMEM((order, wide), F32),
            pltpu.VMEM((1, wide), F32),
            pltpu.VMEM((order, SUB, wide), F32),
            pltpu.VMEM((order, SUB, wide), F32),
            pltpu.VMEM((order, wide), F32),
            pltpu.VMEM((order, wide), F32),
            pltpu.VMEM((nseq, order, wide), F32),
            pltpu.VMEM((4, order, wide), F32),
            pltpu.VMEM((order, wide), F32),
            dma((2, count)), dma((2, count)),
            dma((2, count)), dma((2, count)),
            dma((group,)), dma((group,)),
            dma((2, count)), dma((2, count)),
            dma((nseq,)), dma((nseq,)),
            dma((2,)), dma((2,)),
            dma((nz,)), dma((nz,)),
            dma((2,)), dma((3,)),
            dma((NX + ny - 2, 2, 2)), dma((NX + ny - 2, 2, 2)),
            dma((3,)), dma((3,)),
            dma((2,)), dma((2,)),
            dma((group + 1 + nz,)),
        ],
        compiler_params=pltpu.CompilerParams(
            collective_id=0, has_side_effects=True, vmem_limit_bytes=60 * 1024 * 1024),
        cost_estimate=pl.CostEstimate(flops=flops, bytes_accessed=6 * 1024 * 1024, transcendentals=0),
    )(tokens, w_in.reshape(nchan, width, width), residues.T, decays.T, skip_gain.reshape(1, width), w_out)


def solution(mesh):
    in_specs = (
        P("seq", "chan"),
        P(None, "chan"),
        P("chan", None),
        P("chan", None),
        P("chan"),
        P("chan", None),
    )
    return jax.shard_map(
        functools.partial(per_device, mesh.shape["seq"], mesh.shape["chan"]),
        mesh=mesh, in_specs=in_specs, out_specs=P("seq", "chan"), check_vma=False)
```

time: 409 us -> 99.3 us (0.24); the launches traced: 401 us -> 97.8 us
  waiting for transfers between devices: 176 us -> 0 us
  Pallas kernels: 0 us -> 96 us
  other arithmetic: 87.3 us -> 0 us
  matrix products: 54 us -> 0 us
  starting transfers between devices: 32.7 us -> 0 us
  local copies, waits for them, and re-layouts: 23.9 us -> 1.87 us
  between operations: 13.9 us -> 0.01 us
  blocking collectives: 13.3 us -> 0 us
    pallas_call x0 -> x1, Pallas kernels: none -> 96 us  [per_device(): pl.pallas_call(functools.partial(kernel, nseq, nz, rows, width, order), o...]
    all_gather x1 -> x0, waiting for transfers between devices: 68.7 us -> none  [per_device(): lax.all_gather(tokens, 'chan', axis=1, tiled=True)]
    reduce_scatter x1 -> x0, waiting for transfers between devices: 67.6 us -> none  [per_device(): lax.psum_scatter(lax.dot_general(w_out, conv, (((0,), (1,)), ((), ())), p...]
    sub x16 -> x0, other arithmetic: 66.5 us -> none  [add_order(): return (totals[0] + weighting * den_re, totals[1] - weighting * den_im)]
    dot_general x22 -> x0, matrix products: 54 us -> none  [the longest x4 10.5 us: complex_apply(): jnp.einsum(form, mat_im, vec_re, precision=transform_precision)]
    all_to_all x5 -> x0, waiting for transfers between devices: 38.7 us -> none  [the longest x1 11.6 us: spectral_conv(): lax.all_to_all(turn_re.astype(jnp.bfloat16), 'seq', split_axis=0, concat_...]
    all_to_all x5 -> x0, starting transfers between devices: 32.4 us -> none  [the longest x1 7.27 us: spectral_conv(): lax.all_to_all(stream.reshape(seq_parts, group_rows, channels), 'seq', sp...]
    mul x50 -> x0, other arithmetic: 16 us -> none  [the longest x16 11.7 us: add_order(): lax.dynamic_slice_in_dim(residues, order_idx, 1, 1)[:, 0]]
  transfers between devices with their start and end apart: 7 -> 0, of which waited for: 6 -> 0; matrix products, arithmetic and copies ran while one was open for 25% -> 0% of each run, Pallas kernels for 0% -> 0%
where the time goes in v2:
time: 99.3 us; the launch traced here: 97.8 us
  Pallas kernels  96 us (97%)
  local copies, waits for them, and re-layouts  1.87 us (2%)
    pallas_call x1, Pallas kernels, per_device(): pl.pallas_call(functools.partial(kernel, nseq, nz, rows, width, order), o...  96 us

profile of v2, /device:TPU:6, one launch (start us, length us, event | category | flops | bytes accessed | tf_op | source)
XLA Modules:
  0.0 97.8 jit_solution(8689667467315693830)
XLA Ops:
  0.0 96.0 %shard_map.64 = bf16[1024,256]{1,0:T(8,128)(2,1)} custom-call(bf16[1024,256]{1,0:T(8,128)(2,1)} %tokens.1, bf16[16,256,256]{2,1,0:T(8,128)(2,1)} %bitcast.4, f32[16,256]{1,0:T(8,128)} %bitcast.5, f32[16,256]{1,0:T(8,128)} %bitcast.6, f32[1,256]{1,0:T(1,128)} %bitcast.7, bf16[256,4096]{1,0:T(8,128)(2,1)} %w_out.1), custom_call_target="tpu_custom_call" | custom-call | flops 4294967296 | bytes 6291456 | tf_op jit(solution)/shard_map/pallas_call | solution.py:545
  96.0 1.9 %copy.8 = bf16[1024,256]{1,0:T(8,128)(2,1)} copy(bf16[1024,256]{1,0:T(8,128)(2,1)} %shard_map.64) | data formatting | bytes 1048576

commit v3 on v2

v3 whole, which is shorter than its diff:
```python
import functools

import jax
import jax.numpy as jnp
from jax import lax
from jax.experimental import pallas as pl
from jax.experimental.pallas import tpu as pltpu
from jax.sharding import PartitionSpec as P

MESH = pl.DeviceIdType.MESH
F32 = jnp.float32
BF16 = jnp.bfloat16
SUB = 8
LANES = 128
UNROLL = 8
LAG = 4
SUM_LAG = 4
NX = 4
WI_FIRST, WI_SECOND, WI_RELAY, WI_DONE = 3, 5, 8, 13
WO_START, WO_FIRST, WO_SECOND, WO_RELAY = 5, 9, 12, 17


def hop_counts(nz):
    group = nz // 2
    up, down = {}, {}
    for r in range(nz):
        last = r + group - 1
        if r == 0:
            up[r], down[r] = last, 0
        elif last >= nz:
            up[r], down[r] = last - nz, nz - r
        elif last < nz - r:
            up[r], down[r] = last, 0
        else:
            up[r], down[r] = 0, nz - r
    return up, down


def schedule(lengths, lag):
    left = {r: n for r, n in lengths.items() if n > 0}
    ready = {r: 0 for r in left}
    items, place = [], 0
    while left:
        able = [r for r in left if ready[r] <= place]
        if able:
            r = max(able, key=lambda r: (left[r], -r))
            items.append((r, lengths[r] - left[r] + 1))
            left[r] -= 1
            ready[r] = place + lag
            if left[r] == 0:
                del left[r]
        place += 1
    return items


def paths(nz, lag):
    up, down = hop_counts(nz)
    first = schedule(up, lag)
    mirror = {r: (nz // 2 + 1 - r) % nz for r in range(nz)}
    second = [(mirror[r], h) for r, h in first]
    assert sorted(second) == sorted((r, h) for r in down for h in range(1, down[r] + 1))
    return up, down, (first, second)


def kernel(
    nseq, nz, rows, width, order,
    tokens, w_in, residues_in, decays_in, skip_in, w_out, out,
    x_buf, relay, result, wi_a, wi_b, wo_a, wo_b, acc, u_buf, conv, part, arrived, leaving,
    residues, decays, skip, far_res, far_dec, far_skip, g_buf, d_buf, k_buf, power, before, slot_end, slot_start, last, states, carries, pair_last,
    ring_in, ring_out, pair_in, pair_out, own_in, own_out, sum_in, sum_out, state_in, state_out, conv_in, conv_out,
    wo_in, wo_sent, far_in, far_out, line_in, line_out, pass_in, pass_out, prm_in, prm_out, join_in, join_out, local, own_prm, out_sem,
):
    row = lax.axis_index("seq")
    chan = lax.axis_index("chan")
    z, core = chan // 2, chan % 2
    ny = nseq // NX
    x, y = row // ny, row % ny
    group = nz // 2
    sub = rows // nz
    mine = group * sub
    half = mine // 2
    span = half // SUB
    slot_order = (1, 2, 0, 3) if group == 4 else tuple(range(group))
    per_half = group // 2
    seg = SUB // per_half
    up, down, lists = paths(nz, LAG)
    sum_lists = paths(nz, SUM_LAG)[2]
    count = len(lists[0])
    index = [{item: n for n, item in enumerate(items)} for items in lists]
    sum_index = [{item: n for n, item in enumerate(items)} for items in sum_lists]
    way = (1, -1)

    def at(dz, c):
        return {"chan": 2 * lax.rem(z + dz + nz, nz) + c}

    low_chip = z < group
    near = jnp.where(low_chip, 0, 1)

    ring_dev = [at(1, core), at(nz - 1, core)]
    twin = at(0, 1 - core)
    partner = at(group, core)
    across = at(group, 1 - core)

    barrier = pltpu.get_barrier_semaphore()
    for other in (ring_dev[0], ring_dev[1], twin, partner, across):
        pl.semaphore_signal(barrier, inc=1, device_id=other, device_id_type=MESH)

    def greet(step, _):
        pl.semaphore_signal(
            barrier, inc=1, device_id={"seq": lax.rem(row + step, nseq)}, device_id_type=MESH)
        return 0

    lax.fori_loop(1, nseq, greet, 0)

    def remote(src, dst, send, recv, device):
        return pltpu.make_async_remote_copy(
            src_ref=src, dst_ref=dst, send_sem=send, recv_sem=recv, device_id=device, device_id_type=MESH)

    def slot_of(side, r, h):
        j = (way[side] * h - r) % nz
        return slot_order.index(group - 1 - j) if j < group else None

    def source_block(side, h, c):
        return 2 * lax.rem(z - way[side] * h + 2 * nz, nz) + c

    def slot_rows(k):
        return pl.ds(k * sub, sub)

    relays = [[item for item in lists[side] if slot_of(side, *item) is None] for side in (0, 1)]

    def place_of(side, r, h, block):
        k = slot_of(side, r, h)
        if k is None:
            return relay.at[side, relays[side].index((r, h))]
        return x_buf.at[block, slot_rows(k)]

    def own_rows(r):
        q = lax.rem(z + r, nz)
        return pl.ds(pl.multiple_of(q * sub, sub), sub)

    def ring_copy(side, r, h):
        block = source_block(side, h - 1, core)
        src = tokens.at[own_rows(r)] if h == 1 else place_of(side, r, h - 1, block)
        n = index[side][(r, h)]
        return remote(src, place_of(side, r, h, block), ring_out.at[side, n], ring_in.at[side, n], ring_dev[side])

    def pair_copy(side, r, h, from_twin=False):
        block = source_block(side, h, 1 - core if from_twin else core)
        ref = place_of(side, r, h, block)
        n = index[side][(r, h)]
        return remote(ref, ref, pair_out.at[side, n], pair_in.at[side, n], twin)

    own_parts = [r for r in range(nz) if (-r) % nz < group]

    def own_slot(r):
        return slot_order.index(group - 1 - (-r) % nz)

    def own_load(n):
        r = own_parts[n]
        return pltpu.make_async_copy(
            tokens.at[own_rows(r)], x_buf.at[chan, slot_rows(own_slot(r))], local.at[n])

    def own_pair(n):
        r = own_parts[n]
        return remote(
            tokens.at[own_rows(r)], x_buf.at[chan, slot_rows(own_slot(r))], own_out.at[n], own_in.at[n], twin)

    wi_load = pltpu.make_async_copy(w_in, wi_a, local.at[group])

    far_wi = remote(w_in.at[row], wi_b.at[x, y], far_out.at[0], far_in.at[0], partner)

    def far_wo(c):
        cols = pl.ds(pl.multiple_of((2 * (row // 2) + c) * width, LANES), width)
        device = {"chan": 2 * lax.rem(z + group, nz) + c}
        return remote(w_out.at[:, cols], wo_b.at[x, y], far_out.at[1 + c], far_in.at[1], device)

    low_rows, high_rows = pl.ds(0, width // 2), pl.ds(width // 2, width // 2)

    def lines(which):
        buf = (wi_b, wo_b)[which]
        copies = []
        for step in range(1, NX):
            n = (step - 1, which)
            device = {"seq": lax.rem(x + step, NX) * ny + y}
            ref = buf.at[x, y, low_rows]
            copies.append(remote(ref, ref, line_out.at[n], line_in.at[n], device))
        for step in range(1, ny):
            n = (NX - 1 + step - 1, which)
            device = {"seq": x * ny + lax.rem(y + step, ny)}
            ref = buf.at[x, y, high_rows]
            copies.append(remote(ref, ref, line_out.at[n], line_in.at[n], device))
        return copies

    def pass_on(which, axis, i):
        n, p = ((NX, x), (ny, y))[axis]
        p = lax.rem(p + n + (0, 0, 0, 0, -1, 1)[i], n)
        part_i, step = (0, 1, 1, 0, 0, 1)[i], (1, 1, -1, -1, 1, -1)[i]
        buf = (wi_b, wo_b)[which]
        if axis == 0:
            ref = buf.at[p, pl.ds(part_i * (ny // 2), ny // 2), high_rows]
            device = {"seq": lax.rem(x + step + NX, NX) * ny + y}
        else:
            ref = buf.at[pl.ds(part_i * (NX // 2), NX // 2), p, low_rows]
            device = {"seq": x * ny + lax.rem(y + step + ny, ny)}
        return remote(ref, ref, pass_out.at[which, axis, i], pass_in.at[which, axis, i], device)

    def pass_list(which, name):
        picks = {"own": (0, 2, 1, 3), "first": (0, 2), "on": (4, 5), "rest": (1, 3, 4, 5)}[name]
        short = {"own": (0, 1), "first": (), "on": (), "rest": (0, 1)}[name]
        return [
            pass_on(which, axis, i)
            for place in range(4) for axis in (0, 1)
            for i in ((picks if (NX, ny)[axis] == 4 else short)[place:place + 1])]

    params = [
        remote(src, dst, prm_out.at[n], prm_in.at[n], partner)
        for n, (src, dst) in enumerate(((residues_in, far_res), (decays_in, far_dec), (skip_in, far_skip)))]
    own_params = [
        pltpu.make_async_copy(src, dst, own_prm.at[n])
        for n, (src, dst) in enumerate(((residues_in, residues), (decays_in, decays), (skip_in, skip)))]

    def wo_cols(block, c):
        return pl.ds(pl.multiple_of((2 * block + c) * width, LANES), width)

    def wo_copy(block):
        return remote(
            w_out.at[:, wo_cols(block, 1 - core)], wo_a.at[block, pl.ds(core * width, width)],
            wo_sent.at[block], wo_in.at[block], twin)

    def wo_load(block):
        return pltpu.make_async_copy(
            w_out.at[:, wo_cols(block, core)], wo_a.at[block, pl.ds(core * width, width)],
            local.at[group + 1 + block])

    def half_rows(hf):
        return pl.ds(hf * half, half)

    def project(delta, hf, ab, first):
        total = None
        source = lax.rem(z - delta + nz, nz)
        for c in range(2):
            block = 2 * source + c
            weights = wi_a[block] if ab == 0 else wi_b[block // ny, lax.rem(block, ny)]
            term = jnp.dot(x_buf[block, half_rows(hf)], weights, preferred_element_type=F32)
            total = term if total is None else total + term
        if first:
            acc[ab, half_rows(hf)] = total
        else:
            acc[ab, half_rows(hf)] += total

    cut = jnp.where(low_chip, group - 1 - z, 0)
    sub_id = lax.broadcasted_iota(jnp.int32, (SUB, LANES), 0)
    in_slot = sub_id % seg
    tiles = width // LANES

    def combine(terms):
        while len(terms) > 1:
            terms = [terms[k] + terms[k + 1] if k + 1 < len(terms) else terms[k] for k in range(0, len(terms), 2)]
        return terms[0]

    def scan(turn, tile, hf):
        lanes = pl.ds(tile * LANES, LANES)
        spot = turn * tiles + tile
        ab = jnp.where(low_chip, turn, 1 - turn)
        u_buf[spot, half_rows(hf)] = acc[ab, half_rows(hf), lanes].astype(BF16).astype(F32)
        a = [jnp.broadcast_to(jnp.exp(-d_buf[turn, r:r + 1, lanes]), (SUB, LANES)) for r in range(order)]
        g = [jnp.broadcast_to(g_buf[turn, r:r + 1, lanes], (SUB, LANES)) for r in range(order)]
        direct = jnp.broadcast_to(k_buf[turn, :, lanes], (SUB, LANES))

        def body(i, hs):
            where = pl.ds(hf * half + i, SUB, stride=span)
            u = u_buf[spot, where]
            hs = tuple(a[r] * hs[r] + g[r] * u for r in range(order))
            u_buf[spot, where] = combine([direct * u] + list(hs))
            return hs

        hs = lax.fori_loop(
            0, span, body, tuple(jnp.zeros((SUB, LANES), F32) for _ in range(order)), unroll=UNROLL)
        for r in range(order):
            run = hs[r]
            for shift in (1, 2, 4):
                if shift < seg:
                    factor = jnp.exp(-d_buf[turn, r:r + 1, lanes] * float(span * shift))
                    run = run + jnp.where(in_slot >= shift, factor * pltpu.roll(run, shift, 0), 0.0)
            before[turn, hf, r, :, lanes] = jnp.where(in_slot >= 1, pltpu.roll(run, 1, 0), 0.0)
            for n in range(per_half):
                k = slot_order[hf * per_half + n]
                slot_end[turn, k, r:r + 1, lanes] = run[(n + 1) * seg - 1:(n + 1) * seg]

    early = [(turn, tile) for turn in range(2) for tile in range(tiles)]

    for n in range(group):
        own_load(n).start()
    wi_load.start()
    for copy in own_params:
        copy.start()
    pl.semaphore_wait(barrier, nseq + 4)
    far_wi.start()
    for side in (0, 1):
        ring_copy(side, *lists[side][0]).start()
    for copy in params:
        copy.start()
    for n in range(group):
        own_pair(n).start()

    sources = {}
    for side in (0, 1):
        for n, (r, h) in enumerate(lists[side]):
            if slot_of(side, r, h) is not None:
                sources.setdefault(((way[side] * h) % nz, slot_of(side, r, h) // per_half), []).append((side, r, h, n))
    whole = {key: max(n for _, _, _, n in got) + LAG + 1 for key, got in sources.items()}

    arrived_items, fresh = set(), []

    def arrive(side, r, h):
        if (side, r, h) not in arrived_items:
            arrived_items.add((side, r, h))
            fresh.append((side, r, h))
            ring_copy(side, r, h).wait_recv()

    def hook(place):
        if place == WO_START:
            @pl.when(core == lax.rem(row, 2))
            def _():
                for c in range(2):
                    far_wo(c).start()
        if place == WO_FIRST:
            far_wo(0).wait_recv()
            for copy in lines(1):
                copy.start()
        if place == WO_SECOND:
            for copy in lines(1):
                copy.wait_recv()
            for copy in pass_list(1, "own"):
                copy.start()
        if place == WO_RELAY:
            for copy in pass_list(1, "first"):
                copy.wait_recv()
            for copy in pass_list(1, "on"):
                copy.start()

    far_ready = False
    projected = []
    for step in range(max(count + LAG + 2, WI_DONE + 1)):
        for side in (0, 1):
            if 0 < step < count:
                r, h = lists[side][step]
                if h > 1:
                    arrive(side, r, h - 1)
                ring_copy(side, r, h).start()
        for side in (0, 1):
            if LAG <= step < count + LAG:
                arrive(side, *lists[side][step - LAG])
            for item in list(fresh):
                fresh.remove(item)
                if slot_of(*item) is not None:
                    pair_copy(*item).start()
        if step == 1:
            for block in range(nz):
                wo_load(block).start()
                wo_copy(block).start()
        if step == 2:
            for n in range(group):
                own_load(n).wait()
                own_pair(n).wait_recv()
            wi_load.wait()
            for hf in range(2):
                project(0, hf, 0, True)
                projected.append((0, hf))
        hook(step)
        if step == WI_FIRST:
            far_wi.wait_recv()
            for copy in lines(0):
                copy.start()
        if step == WI_SECOND:
            for copy in lines(0):
                copy.wait_recv()
            for copy in pass_list(0, "own"):
                copy.start()
        if step == WI_RELAY:
            for copy in pass_list(0, "first"):
                copy.wait_recv()
            for copy in pass_list(0, "on"):
                copy.start()
        if step == WI_DONE:
            for copy in pass_list(0, "rest"):
                copy.wait_recv()
            far_ready = True
            for delta, hf in projected:
                project(delta, hf, 1, delta == 0)
            for copy in params:
                copy.wait_recv()
            for copy in own_params:
                copy.wait()
            g_buf[near] = residues[...] * jnp.sqrt(decays[...])
            g_buf[1 - near] = far_res[...] * jnp.sqrt(far_dec[...])
            d_buf[near] = decays[...]
            d_buf[1 - near] = far_dec[...]
            k_buf[near] = skip[...]
            k_buf[1 - near] = far_skip[...]
        for key, ready in whole.items():
            if ready == step:
                for side, r, h, _ in sources[key]:
                    pair_copy(side, r, h, True).wait_recv()
                project(*key, 0, False)
                if far_ready:
                    project(*key, 1, False)
                projected.append(key)
        if far_ready and len([1 for _, hf in projected if hf == 0]) == nz and early:
            scan(*early.pop(0), 0)
    assert far_ready and len(projected) == 2 * nz
    for turn, tile in early:
        scan(turn, tile, 0)

    def decay_over(turn, parts):
        return jnp.exp(-d_buf[turn] * (parts * sub).astype(F32))

    def state_copy(turn, src, target):
        return remote(
            states.at[turn, src], states.at[turn, src], state_out.at[turn, target], state_in.at[turn, src],
            {"seq": target})

    def join_last(turn):
        return remote(last.at[turn], pair_last.at[turn], join_out.at[turn, 0], join_in.at[turn, 0], partner)

    def join_carry(turn):
        return remote(
            carries.at[turn, 0], carries.at[turn, 1], join_out.at[turn, 1], join_in.at[turn, 1], partner)

    for turn in range(2):
        hook(100 + turn)
        for tile in range(tiles):
            scan(turn, tile, 1)
        slot_decay = jnp.exp(-d_buf[turn] * float(sub))
        run = tail = jnp.zeros((order, width), F32)
        for k in range(group):
            run = jnp.where(cut == k, 0.0, run * slot_decay) + slot_end[turn, k]
            tail = jnp.where(cut == k + 1, run, tail)
        last[turn] = run
        states[turn, row] = decay_over(turn, nz - 1 - z) * run + tail

        def send_state(target, _, turn=turn):
            state_copy(turn, row, target).start()
            return 0

        lax.fori_loop(row + 1, nseq, send_state, 0)
        join_last(turn).start()

    def get_carry(turn):
        block_decay = jnp.exp(-d_buf[turn] * float(rows))

        def add_state(src, carry):
            state_copy(turn, src, row).wait_recv()
            return block_decay * carry + states[turn, src]

        carries[turn, 0] = lax.fori_loop(0, row, add_state, jnp.zeros((order, width), F32))
        join_carry(turn).start()

    def set_powers(turn):
        for tile in range(tiles):
            lanes = pl.ds(tile * LANES, LANES)
            for r in range(order):
                power[turn, r, :, lanes] = jnp.exp(
                    -d_buf[turn, r:r + 1, lanes] * (in_slot.astype(F32) * float(span)))

    def join(turn):
        to_middle = decay_over(turn, jnp.where(low_chip, z + 1, z - group + 1))
        to_end = jnp.exp(-d_buf[turn] * float(group * sub))
        join_last(turn).wait_recv()
        join_carry(turn).wait_recv()
        carry = carries[turn, 0] + carries[turn, 1]
        middle = to_middle * carry + jnp.where(low_chip, last[turn], pair_last[turn])
        begin = jnp.where(low_chip, carry, middle)
        slot_decay = jnp.exp(-d_buf[turn] * float(sub))
        ahead = jnp.where(cut > 0, to_end * middle + pair_last[turn], begin)
        for k in range(group):
            if k > 0:
                ahead = jnp.where(cut == k, begin, ahead * slot_decay + slot_end[turn, k - 1])
            slot_start[turn, k] = ahead

    def finish(turn, tile, hf):
        lanes = pl.ds(tile * LANES, LANES)
        spot = turn * tiles + tile
        a = [jnp.broadcast_to(jnp.exp(-d_buf[turn, r:r + 1, lanes]), (SUB, LANES)) for r in range(order)]
        hs = []
        for r in range(order):
            start = None
            for n in range(per_half):
                value = slot_start[turn, slot_order[hf * per_half + n], r:r + 1, lanes]
                start = value if start is None else jnp.where(sub_id >= n * seg, value, start)
            hs.append(before[turn, hf, r, :, lanes] + power[turn, r, :, lanes] * start)

        def body(i, hs):
            where = pl.ds(hf * half + i, SUB, stride=span)
            hs = tuple(a[r] * hs[r] for r in range(order))
            u_buf[spot, where] = combine([u_buf[spot, where]] + list(hs))
            return hs

        lax.fori_loop(0, span, body, tuple(hs), unroll=UNROLL)
        conv[core, turn, half_rows(hf), lanes] = u_buf[spot, half_rows(hf)].astype(BF16)

    def conv_copy(turn, hf, c):
        ref = conv.at[c, turn, half_rows(hf)]
        return remote(ref, ref, conv_out.at[turn, hf], conv_in.at[turn, hf], twin)

    for turn in range(2):
        hook(102 + turn)
        set_powers(turn)
    for turn in range(2):
        get_carry(turn)
        hook(104 + turn)
    for turn in range(2):
        join(turn)
        for hf in (1, 0):
            for tile in range(tiles):
                finish(turn, tile, hf)
            conv_copy(turn, hf, core).start()

    def part_terms(delta, hf, c):
        block = lax.rem(z - delta + nz, nz)
        share = 2 * block + c
        return jnp.dot(
            conv[c, near, half_rows(hf)], wo_a[block, pl.ds(c * width, width)], preferred_element_type=F32) + jnp.dot(
            conv[c, 1 - near, half_rows(hf)], wo_b[share // ny, lax.rem(share, ny)], preferred_element_type=F32)

    for block in range(nz):
        wo_load(block).wait()
        wo_copy(block).wait_recv()
    for copy in pass_list(1, "rest"):
        copy.wait_recv()

    def target_of(side, r, i):
        length = (up, down)[side][r]
        h = length - i + 1
        return (way[side] * h) % nz, slot_of(side, r, h)

    def sum_copy(side, r, i):
        n = sum_index[side][(r, i)]
        delta, k = target_of(side, r, i)
        src = arrived.at[side, sum_index[side][(r, i - 1)]] if k is None else leaving.at[side, n]
        return remote(src, arrived.at[side, n], sum_out.at[side, n], sum_in.at[side, n], ring_dev[1 - side])

    have, seen = set(), set()

    def need(delta, k):
        hf = k // per_half
        if hf not in seen:
            seen.add(hf)
            for turn in range(2):
                conv_copy(turn, hf, 1 - core).wait_recv()
        if (delta, hf) not in have:
            have.add((delta, hf))
            part[delta, half_rows(hf)] = part_terms(delta, hf, 0) + part_terms(delta, hf, 1)

    def out_copy(r):
        return pltpu.make_async_copy(result.at[r], out.at[own_rows(r)], out_sem.at[r])

    def finish_sum(r):
        total = None
        if (-r) % nz < group:
            need(0, own_slot(r))
            total = part[0, slot_rows(own_slot(r))]
        for side in (0, 1):
            length = (up, down)[side][r]
            if length > 0:
                sum_copy(side, r, length).wait_recv()
                got = arrived[side, sum_index[side][(r, length)]].astype(F32)
                total = got if total is None else total + got
        result[r] = total.astype(BF16)
        out_copy(r).start()

    drains = []
    for side in (0, 1):
        for item in lists[side]:
            drains.append(ring_copy(side, *item).wait_send)
            if slot_of(side, *item) is not None:
                drains.append(pair_copy(side, *item).wait_send)
    drains += [own_pair(n).wait_send for n in range(group)] + [far_wi.wait_send]
    for which in range(2):
        drains += [copy.wait_send for copy in lines(which) + pass_list(which, "own") + pass_list(which, "on")]
    drains += [copy.wait_send for copy in params]
    drains += [wo_copy(block).wait_send for block in range(nz)]
    for turn in range(2):
        drains += [join_last(turn).wait_send, join_carry(turn).wait_send]
        drains += [conv_copy(turn, hf, core).wait_send for hf in range(2)]

    def drain_far():
        @pl.when(core == lax.rem(row, 2))
        def _():
            for c in range(2):
                far_wo(c).wait_send()

    def drain_states():
        def one(target, _):
            for turn in range(2):
                state_copy(turn, row, target).wait_send()
            return 0

        lax.fori_loop(row + 1, nseq, one, 0)

    drains += [drain_far, drain_states]
    batch = -(-len(drains) // (count - 2))

    ends = {r: max([sum_index[s][(r, (up, down)[s][r])] for s in (0, 1) if (up, down)[s][r] > 0] + [0]) + SUM_LAG for r in range(nz)}
    for step in range(count + SUM_LAG + 1):
        for side in (0, 1):
            if step < count:
                r, i = sum_lists[side][step]
                delta, k = target_of(side, r, i)
                if k is not None:
                    need(delta, k)
                if i > 1:
                    sum_copy(side, r, i - 1).wait_recv()
                if k is not None:
                    value = part[delta, slot_rows(k)]
                    if i > 1:
                        value = value + arrived[side, sum_index[side][(r, i - 1)]].astype(F32)
                    leaving[side, sum_index[side][(r, i)]] = value.astype(BF16)
                sum_copy(side, r, i).start()
        if step > 0:
            for wait in drains[:batch]:
                wait()
            del drains[:batch]
        for r in range(nz):
            if ends[r] == step:
                finish_sum(r)

    for side in (0, 1):
        for item in sum_lists[side]:
            sum_copy(side, *item).wait_send()
    for r in range(nz):
        out_copy(r).wait()
    assert not drains


def per_device(nseq, nchan, tokens, w_in, residues, decays, skip_gain, w_out):
    rows, width = tokens.shape
    order = residues.shape[1]
    nz = nchan // 2
    ny = nseq // NX
    group = nz // 2
    mine = rows // 2
    count = len(paths(nz, LAG)[2][0])
    dma = pltpu.SemaphoreType.DMA
    hbm = pl.BlockSpec(memory_space=pl.ANY)
    flops = 4 * rows * width * nchan * width
    return pl.pallas_call(
        functools.partial(kernel, nseq, nz, rows, width, order),
        out_shape=jax.ShapeDtypeStruct((rows, width), BF16),
        in_specs=[hbm] * 6,
        out_specs=hbm,
        scratch_shapes=[
            pltpu.VMEM((nchan, mine, width), BF16),
            pltpu.VMEM((2, 1, rows // nz, width), BF16),
            pltpu.VMEM((nz, rows // nz, width), BF16),
            pltpu.VMEM((nchan, width, width), BF16),
            pltpu.VMEM((NX, ny, width, width), BF16),
            pltpu.VMEM((nz, 2 * width, width), BF16),
            pltpu.VMEM((NX, ny, width, width), BF16),
            pltpu.VMEM((2, mine, width), F32),
            pltpu.VMEM((2 * width // LANES, mine, LANES), F32),
            pltpu.VMEM((2, 2, mine, width), BF16),
            pltpu.VMEM((nz, mine, width), F32),
            pltpu.VMEM((2, count, rows // nz, width), BF16),
            pltpu.VMEM((2, count, rows // nz, width), BF16),
            pltpu.VMEM((order, width), F32),
            pltpu.VMEM((order, width), F32),
            pltpu.VMEM((1, width), F32),
            pltpu.VMEM((order, width), F32),
            pltpu.VMEM((order, width), F32),
            pltpu.VMEM((1, width), F32),
            pltpu.VMEM((2, order, width), F32),
            pltpu.VMEM((2, order, width), F32),
            pltpu.VMEM((2, 1, width), F32),
            pltpu.VMEM((2, order, SUB, width), F32),
            pltpu.VMEM((2, 2, order, SUB, width), F32),
            pltpu.VMEM((2, group, order, width), F32),
            pltpu.VMEM((2, group, order, width), F32),
            pltpu.VMEM((2, order, width), F32),
            pltpu.VMEM((2, nseq, order, width), F32),
            pltpu.VMEM((2, 2, order, width), F32),
            pltpu.VMEM((2, order, width), F32),
            dma((2, count)), dma((2, count)),
            dma((2, count)), dma((2, count)),
            dma((group,)), dma((group,)),
            dma((2, count)), dma((2, count)),
            dma((2, nseq)), dma((2, nseq)),
            dma((2, 2)), dma((2, 2)),
            dma((nz,)), dma((nz,)),
            dma((2,)), dma((3,)),
            dma((NX + ny - 2, 2)), dma((NX + ny - 2, 2)),
            dma((2, 2, 6)), dma((2, 2, 6)),
            dma((3,)), dma((3,)),
            dma((2, 2)), dma((2, 2)),
            dma((group + 1 + nz,)),
            dma((3,)),
            dma((nz,)),
        ],
        compiler_params=pltpu.CompilerParams(
            collective_id=0, has_side_effects=True, vmem_limit_bytes=56 * 1024 * 1024),
        cost_estimate=pl.CostEstimate(flops=flops, bytes_accessed=6 * 1024 * 1024, transcendentals=0),
    )(tokens, w_in.reshape(nchan, width, width), residues.T, decays.T, skip_gain.reshape(1, width), w_out)


def solution(mesh):
    in_specs = (
        P("seq", "chan"),
        P(None, "chan"),
        P("chan", None),
        P("chan", None),
        P("chan"),
        P("chan", None),
    )
    return jax.shard_map(
        functools.partial(per_device, mesh.shape["seq"], mesh.shape["chan"]),
        mesh=mesh, in_specs=in_specs, out_specs=P("seq", "chan"), check_vma=False)
```

time: 99.3 us -> 95.6 us (0.963); the launches traced: 97.8 us -> 95.5 us
  Pallas kernels: 96 us -> 93.6 us
    pallas_call x1, Pallas kernels: 96 us -> 93.6 us  [per_device(): pl.pallas_call(functools.partial(kernel, nseq, nz, rows, width, order), o...]
where the time goes in v3:
time: 95.6 us; the launch traced here: 95.5 us
  Pallas kernels  93.6 us (98%)
  local copies, waits for them, and re-layouts  1.87 us (2%)
    pallas_call x1, Pallas kernels, per_device(): pl.pallas_call(functools.partial(kernel, nseq, nz, rows, width, order), o...  93.6 us

profile of v3, /device:TPU:6, one launch (start us, length us, event | category | flops | bytes accessed | tf_op | source)
XLA Modules:
  0.0 95.5 jit_solution(11783912188340177234)
XLA Ops:
  0.0 93.6 %shard_map.64 = bf16[1024,256]{1,0:T(8,128)(2,1)} custom-call(bf16[1024,256]{1,0:T(8,128)(2,1)} %tokens.1, bf16[16,256,256]{2,1,0:T(8,128)(2,1)} %bitcast.4, f32[16,256]{1,0:T(8,128)} %bitcast.5, f32[16,256]{1,0:T(8,128)} %bitcast.6, f32[1,256]{1,0:T(1,128)} %bitcast.7, bf16[256,4096]{1,0:T(8,128)(2,1)} %w_out.1), custom_call_target="tpu_custom_call" | custom-call | flops 4294967296 | bytes 6291456 | tf_op jit(solution)/shard_map/pallas_call | solution.py:647
  93.6 1.9 %copy.8 = bf16[1024,256]{1,0:T(8,128)(2,1)} copy(bf16[1024,256]{1,0:T(8,128)(2,1)} %shard_map.64) | data formatting | bytes 1048576

commit v4 on v3

--- a/solution.py
+++ b/solution.py
@@ -12,9 +12,9 @@
 BF16 = jnp.bfloat16
 SUB = 8
 LANES = 128
-UNROLL = 8
+UNROLL = 16
 LAG = 4
-SUM_LAG = 4
+SUM_LAG = 6
 NX = 4
 WI_FIRST, WI_SECOND, WI_RELAY, WI_DONE = 3, 5, 8, 13
 WO_START, WO_FIRST, WO_SECOND, WO_RELAY = 5, 9, 12, 17
@@ -298,8 +298,6 @@
     far_wi.start()
     for side in (0, 1):
         ring_copy(side, *lists[side][0]).start()
-    for copy in params:
-        copy.start()
     for n in range(group):
         own_pair(n).start()
 
@@ -356,6 +354,9 @@
                 if slot_of(*item) is not None:
                     pair_copy(*item).start()
         if step == 1:
+            for copy in params:
+                copy.start()
+        if step == 6:
             for block in range(nz):
                 wo_load(block).start()
                 wo_copy(block).start()
@@ -511,7 +512,7 @@
         hook(104 + turn)
     for turn in range(2):
         join(turn)
-        for hf in (1, 0):
+        for hf in (0, 1):
             for tile in range(tiles):
                 finish(turn, tile, hf)
             conv_copy(turn, hf, core).start()

time: 95.6 us -> 95.6 us (level)
  no operation moved by 1% of the time
where the time goes in v4:
time: 95.6 us; the launch traced here: 95 us
  Pallas kernels  93.1 us (97%)
  local copies, waits for them, and re-layouts  1.87 us (2%)
    pallas_call x1, Pallas kernels, per_device(): pl.pallas_call(functools.partial(kernel, nseq, nz, rows, width, order), o...  93.1 us

profile of v4, /device:TPU:6, one launch (start us, length us, event | category | flops | bytes accessed | tf_op | source)
XLA Modules:
  0.0 95.0 jit_solution(13013079776503051210)
XLA Ops:
  0.0 93.1 %shard_map.64 = bf16[1024,256]{1,0:T(8,128)(2,1)} custom-call(bf16[1024,256]{1,0:T(8,128)(2,1)} %tokens.1, bf16[16,256,256]{2,1,0:T(8,128)(2,1)} %bitcast.4, f32[16,256]{1,0:T(8,128)} %bitcast.5, f32[16,256]{1,0:T(8,128)} %bitcast.6, f32[1,256]{1,0:T(1,128)} %bitcast.7, bf16[256,4096]{1,0:T(8,128)(2,1)} %w_out.1), custom_call_target="tpu_custom_call" | custom-call | flops 4294967296 | bytes 6291456 | tf_op jit(solution)/shard_map/pallas_call | solution.py:648
  93.1 1.9 %copy.8 = bf16[1024,256]{1,0:T(8,128)(2,1)} copy(bf16[1024,256]{1,0:T(8,128)(2,1)} %shard_map.64) | data formatting | bytes 1048576
